TPU v7x, 32 devices: a whole 2x2x4 slice. The times are simulated.
32 devices in a mesh: ctx: 8 (over z, x), section: 4 (over y, core).
Axes of the slice: x: 2, y: 2, z: 4, core: 2. Of those that a mesh axis runs over, the one named last changes fastest.
Arguments:
- query_heads: bfloat16 [4, 1024, 4096], P('section', 'ctx'), may hold values from -12 to 12
- key_heads: bfloat16 [4, 1024, 512], P('section', 'ctx'), may hold values from -12 to 12
- value_heads: bfloat16 [4, 1024, 512], P('section', 'ctx'), may hold values from -6 to 6
- attn_output: bfloat16 [4, 1024, 4096], P('section', 'ctx'), may hold values from -6 to 6
- output_grad: bfloat16 [4, 1024, 4096], P('section', 'ctx'), may hold values from -6 to 6
- doc_start: int32 [1024], P('ctx'), may hold values from 0 to 1023, as said below
- fetch_list: int32 [8, 2], P('ctx'), may hold values from 0 to 1, as said below
Outputs:
- handed_grad: bfloat16 [4, 1024, 4096], P('section', 'ctx')
- key_grad: bfloat16 [4, 1024, 512], P('section', 'ctx')
- value_grad: bfloat16 [4, 1024, 512], P('section', 'ctx')
Inputs may be any that keep to these rules, and one draw needn't show every extreme that they name: doc_start never falls, doc_start[t] <= t, and positions with equal doc_start form one document; a document holds at most 257 positions, and some hold exactly that many; the last position forms a document of its own. fetch_list[i, d - 1] is 1 exactly when some position of shard i and some position of shard i - d lie in one document.
All inputs are finite; a program needn't handle non-finite values.
Results may differ from a plain program's by a relative error of at most 0.0095.
Values may be sent and summed in bfloat16 or wider, within the bound.
No kernel may reach another device: no remote copies, remote signals or barrier semaphores. Data moves between devices by JAX's collectives and lax.ppermute only.
A program may use at most 64 MiB of HBM per device.

v0:
```python
import math

import jax
import jax.numpy as jnp
from jax import lax
from jax.sharding import PartitionSpec as P

HQ = 32
HK = 4
HD = 128
FETCH = 2


ROPE_BASE = 1000000.0
TRAINED_CONTEXT = 32768.0
YARN_FACTOR = 4.0
NEG_LARGE = -1e30


def from_behind(value, axis, steps):
    count = lax.axis_size(axis)
    initial, last = (max(0, -steps), min(count, count - steps))
    return lax.ppermute(value, axis, [(source, source + steps) for source in range(initial, last)])


def yarn_frequencies(head_dim):
    half_dim = head_dim // 2

    def correction(rotations):
        return (
            head_dim
            * math.log(TRAINED_CONTEXT / (rotations * 2.0 * math.pi))
            / (2.0 * math.log(ROPE_BASE))
        )

    lower_dim = max(math.floor(correction(32.0)), 0)
    upper_dim = min(math.ceil(correction(1.0)), head_dim - 1)
    spread_dims = max(upper_dim - lower_dim, 0.001)
    indices = jnp.arange(half_dim, dtype=jnp.float32)
    extrapolated = jnp.power(jnp.float32(ROPE_BASE), -2.0 * indices / head_dim)
    ramp_weight = jnp.clip((indices - lower_dim) / spread_dims, 0.0, 1.0)
    return extrapolated / YARN_FACTOR * ramp_weight + extrapolated * (1.0 - ramp_weight)


def rope_tables(positions, head_dim):
    freqs = yarn_frequencies(head_dim)
    angles = positions.astype(jnp.float32)[:, None] * freqs[None, :]
    angles = jnp.concatenate([angles, angles], axis=1)
    factor = 0.1 * math.log(YARN_FACTOR) + 1.0
    return ((jnp.cos(angles) * factor)[:, None, :], (jnp.sin(angles) * factor)[:, None, :])


def apply_rope(inputs, cosine, sine_table):
    half_dim = inputs.shape[-1] // 2
    turned = jnp.concatenate([-inputs[..., half_dim:], inputs[..., :half_dim]], axis=-1)
    return inputs * cosine + turned * sine_table


def undo_rope(grads, cosine, sine_table):
    half_dim = grads.shape[-1] // 2
    scaled = grads * sine_table
    return grads * cosine + jnp.concatenate(
        [scaled[..., half_dim:], -scaled[..., :half_dim]], axis=-1
    )


def shards(query_heads, key_heads, value_heads, attn_output, output_grad, doc_start, fetch_list):
    tok_rows = query_heads.shape[1]
    ratio = HQ // HK
    score_scale = HD ** (-0.5)
    first_row = lax.axis_index("ctx") * tok_rows
    block_idx = jnp.arange(tok_rows, dtype=jnp.int32)
    t_pos = first_row + block_idx
    cosine, sine_table = rope_tables(t_pos - doc_start, HD)
    q_rot = apply_rope(
        query_heads[0].astype(jnp.float32).reshape(tok_rows, HQ, HD), cosine, sine_table
    )
    q_rot = q_rot.astype(jnp.bfloat16).reshape(tok_rows, HK, ratio, HD)
    k_rot = apply_rope(
        key_heads[0].astype(jnp.float32).reshape(tok_rows, HK, HD), cosine, sine_table
    ).astype(jnp.bfloat16)
    val_rows = value_heads[0].reshape(tok_rows, HK, HD)
    grad_rows = output_grad[0].reshape(tok_rows, HK, ratio, HD)
    delta = jnp.sum(
        (output_grad[0].astype(jnp.float32) * attn_output[0].astype(jnp.float32)).reshape(
            tok_rows, HK, ratio, HD
        ),
        axis=-1,
    )
    listed = fetch_list[0]
    blocks = [(k_rot, val_rows)]
    for distance in range(1, FETCH + 1):
        blocks.append(from_behind((k_rot, val_rows), "ctx", distance))
    masks = []
    for distance in range(FETCH + 1):
        u_pos = first_row - distance * tok_rows + block_idx
        masks.append((u_pos[None, :] >= doc_start[:, None]) & (u_pos[None, :] <= t_pos[:, None]))
    stat_shape = (tok_rows, HK, ratio)
    empty_stats = (jnp.full(stat_shape, NEG_LARGE, jnp.float32), jnp.zeros(stat_shape, jnp.float32))

    def tile_stats(k_blk, allowed):
        scores = (
            jnp.einsum("tgre,uge->tgru", q_rot, k_blk, preferred_element_type=jnp.float32)
            * score_scale
        )
        pair_mask = allowed[:, None, None, :]
        largest = jnp.max(jnp.where(pair_mask, scores, NEG_LARGE), axis=-1)
        exp_total = jnp.sum(
            jnp.where(pair_mask, jnp.exp(scores - largest[..., None]), 0.0), axis=-1
        )
        return (largest, exp_total)

    all_stats = [tile_stats(blocks[0][0], masks[0])]
    for distance in range(1, FETCH + 1):
        all_stats.append(
            lax.cond(
                listed[distance - 1] == 1,
                lambda k_blk=blocks[distance][0], allowed=masks[distance]: tile_stats(
                    k_blk, allowed
                ),
                lambda: empty_stats,
            )
        )
    overall = all_stats[0][0]
    for stats in all_stats[1:]:
        overall = jnp.maximum(overall, stats[0])
    summed = jnp.zeros(stat_shape, jnp.float32)
    for stats in all_stats:
        summed = summed + stats[1] * jnp.exp(stats[0] - overall)
    lse = overall + jnp.log(summed)

    def tile_grads(k_blk, v_blk, allowed):
        scores = (
            jnp.einsum("tgre,uge->tgru", q_rot, k_blk, preferred_element_type=jnp.float32)
            * score_scale
        )
        pair_mask = allowed[:, None, None, :]
        prob = jnp.where(pair_mask, jnp.exp(scores - lse[..., None]), 0.0)
        prob_b = prob.astype(jnp.bfloat16)
        dprob = jnp.einsum("tgre,uge->tgru", grad_rows, v_blk, preferred_element_type=jnp.float32)
        dscore = (prob * (dprob - delta[..., None])).astype(jnp.bfloat16)
        dq_part = (
            jnp.einsum("tgru,uge->tgre", dscore, k_blk, preferred_element_type=jnp.float32)
            * score_scale
        )
        dk_part = (
            jnp.einsum("tgru,tgre->uge", dscore, q_rot, preferred_element_type=jnp.float32)
            * score_scale
        )
        dv_part = jnp.einsum(
            "tgru,tgre->uge", prob_b, grad_rows, preferred_element_type=jnp.float32
        )
        return (dq_part, dk_part, dv_part)

    zero_kv = jnp.zeros((tok_rows, HK, HD), jnp.float32)
    empty_grads = (jnp.zeros((tok_rows, HK, ratio, HD), jnp.float32), zero_kv, zero_kv)
    own_grads = tile_grads(blocks[0][0], blocks[0][1], masks[0])
    dq_sum = own_grads[0]
    contributions = [(own_grads[1], own_grads[2])]
    for distance in range(1, FETCH + 1):
        tile_result = lax.cond(
            listed[distance - 1] == 1,
            lambda k_blk=blocks[distance][0], v_blk=blocks[distance][1], allowed=masks[
                distance
            ]: tile_grads(k_blk, v_blk, allowed),
            lambda: empty_grads,
        )
        dq_sum = dq_sum + tile_result[0]
        contributions.append((tile_result[1], tile_result[2]))
    returned = (zero_kv, zero_kv)
    for distance in range(1, FETCH + 1):
        arrived = from_behind(contributions[distance], "ctx", -distance)
        returned = (returned[0] + arrived[0], returned[1] + arrived[1])
    dk_total = contributions[0][0] + returned[0]
    dv_total = contributions[0][1] + returned[1]
    key_grad = (
        undo_rope(dk_total, cosine, sine_table).astype(jnp.bfloat16).reshape(1, tok_rows, HK * HD)
    )
    value_grad = dv_total.astype(jnp.bfloat16).reshape(1, tok_rows, HK * HD)
    query_grad = (
        undo_rope(dq_sum.reshape(tok_rows, HQ, HD), cosine, sine_table)
        .astype(jnp.bfloat16)
        .reshape(1, tok_rows, HQ * HD)
    )
    handed_grad = from_behind(query_grad, "section", -1)
    return (handed_grad, key_grad, value_grad)


def solution(mesh):
    return jax.shard_map(
        shards,
        mesh=mesh,
        in_specs=(
            P("section", "ctx", None),
            P("section", "ctx", None),
            P("section", "ctx", None),
            P("section", "ctx", None),
            P("section", "ctx", None),
            P("ctx"),
            P("ctx", None),
        ),
        out_specs=(P("section", "ctx", None), P("section", "ctx", None), P("section", "ctx", None)),
        check_vma=False,
    )
```

profile of v0, /device:TPU:21, one launch (start us, length us, event | category | flops | bytes accessed | tf_op | source)
XLA Modules:
  0.0 114.9 jit_solution(14205346651300604726)
XLA Ops:
  3.5 3.2 %collective-permute-start.1 = (bf16[128,4,128]{0,2,1:T(8,128)(2,1)}, bf16[128,4,128]{0,2,1:T(8,128)(2,1)S(1)}, u32[]{:S(2)}, u32[]{:S(2)}) collective-permute-start(bf16[128,4,128]{0,2,1:T(8,128)(2,1)} %fusion.53), channel_id=1, source_target_pairs={{0,8},{4,12},{8,16},{12,20},{16,24},{20,28},{1,9},{5,13},{9,17},{1... | collective-permute-start | bytes 393224 | tf_op jit(solution)/shard_map/ppermute | solution.py:23
  6.7 3.1 %collective-permute-start = (bf16[128,4,128]{0,2,1:T(8,128)(2,1)}, bf16[128,4,128]{0,2,1:T(8,128)(2,1)S(1)}, u32[]{:S(2)}, u32[]{:S(2)}) collective-permute-start(bf16[128,4,128]{0,2,1:T(8,128)(2,1)} %fusion.53), channel_id=1, source_target_pairs={{0,4},{4,8},{8,12},{12,16},{16,20},{20,24},{24,28},{1,5},{5,9},{9,... | collective-permute-start | bytes 393224 | tf_op jit(solution)/shard_map/ppermute | solution.py:23
  13.4 1.9 %collective-permute-start.2 = (bf16[128,4,128]{0,2,1:T(8,128)(2,1)}, bf16[128,4,128]{0,2,1:T(8,128)(2,1)}, u32[]{:S(2)}, u32[]{:S(2)}) collective-permute-start(bf16[128,4,128]{0,2,1:T(8,128)(2,1)} %bitcast.37), channel_id=1, source_target_pairs={{0,4},{4,8},{8,12},{12,16},{16,20},{20,24},{24,28},{1,5},{5,9},{9,... | collective-permute-start | bytes 393224 | tf_op jit(solution)/shard_map/ppermute | solution.py:23
  25.6 2.7 %fusion.33 = bf16[128,4,8,128]{0,3,2,1:T(8,128)(2,1)S(1)} fusion(f32[128,4,8,64]{0,3,2,1:T(8,128)} %bitcast.230, f32[128,4,8,64]{0,3,2,1:T(8,128)} %bitcast.229, f32[128,4,8,128]{0,3,2,1:T(8,128)} %bitcast.225, f32[128,128]{0,1:T(8,128)S(1)} %get-tuple-element.167, f32[128,128]{0,1:T(8,128)S(1)} %get-tuple-element.166), kind=kLoop, calls=%fused_computation.48 | loop fusion | flops 2621440 | bytes 5373952 | tf_op jit(solution)/shard_map/convert_element_type | solution.py:78
  31.1 2.3 %conditional.5 = (f32[128,4,8]{0,2,1:T(8,128)}, f32[128,4,8]{0,2,1:T(8,128)S(1)}) conditional(s32[]{:T(128)} %bitcast.36, () %tuple.42, (pred[128,128]{0,1:T(8,128)(4,1)S(1)}, bf16[128,4,128]{0,2,1:T(8,128)(2,1)S(1)}, bf16[128,4,8,128]{0,3,2,1:T(8,128)(2,1)S(1)}) %tuple.43), branch_computations={%region_5.6_spmd, %region_6.9_spmd} | conditional | flops 137879552 | bytes 5455888 | solution.py:116
  33.4 2.3 %conditional.4 = (f32[128,4,8]{0,2,1:T(8,128)}, f32[128,4,8]{0,2,1:T(8,128)S(1)}) conditional(s32[]{:T(128)} %bitcast.35, () %tuple.40, (pred[128,128]{0,1:T(8,128)(4,1)S(1)}, bf16[128,4,128]{0,2,1:T(8,128)(2,1)S(1)}, bf16[128,4,8,128]{0,3,2,1:T(8,128)(2,1)S(1)}) %tuple.41), branch_computations={%region_1.2_spmd, %region_2.0_spmd} | conditional | flops 137879552 | bytes 5455888 | solution.py:116
  36.5 2.3 %fusion.37 = bf16[128,4,8,128]{0,3,2,1:T(8,128)(2,1)S(1)} fusion(bf16[128,4,128,1]{0,2,3,1:T(8,128)(2,1)} %bitcast.71, bf16[128,4,8,128]{0,3,2,1:T(8,128)(2,1)S(1)} %bitcast.220, f32[4,128,128,8]{2,1,3,0:T(8,128)} %copy-done, f32[128,4,8]{0,2,1:T(8,128)S(1)} %fusion.34, f32[128,4,8]{0,2,1:T(8,128)S(1)} %log_add_fusion, pred[128,128]{0,1:T(8,128)(4,1)} %copy-done.7), kind=kOutput, calls=%fused_computation.57 | convolution fusion | flops 137363456 | bytes 4374528 | tf_op jit(solution)/shard_map/tgre,uge->tgru/dot_general | solution.py:140
  38.9 2.7 %fusion.57 = f32[4,128,128,8]{2,1,3,0:T(8,128)} fusion(bf16[128,4,8,128]{0,3,2,1:T(8,128)(2,1)S(1)} %fusion.37, bf16[128,4,128]{0,2,1:T(8,128)(2,1)} %fusion.53), kind=kOutput, calls=%fused_computation.90 | convolution fusion | flops 134217728 | bytes 3276800 | tf_op jit(solution)/shard_map/tgru,uge->tgre/dot_general | solution.py:143
  41.6 9.2 %conditional.7 = (f32[128,4,128]{2,0,1:T(8,128)}, f32[128,4,128]{2,0,1:T(8,128)}, f32[128,4,8,128]{0,3,2,1:T(8,128)}) conditional(s32[]{:T(128)} %bitcast.36, () %tuple.46, (pred[128,128]{0,1:T(8,128)(4,1)S(1)}, bf16[128,4,128]{0,2,1:T(8,128)(2,1)S(1)}, bf16[128,4,8,128]{0,3,2,1:T(8,128)(2,1)S(1)}, f32[128,4,8]{0,2,1:T(8,128)S(1)}, ...), branch_computations={%region_13.14_spmd, %region_14.15_spmd} | conditional | flops 675348480 | bytes 20889624 | solution.py:161
  45.9 1.9 %multiply_bitcast_fusion.1 = f32[128,4,8,128]{3,0,2,1:T(8,128)} fusion(bf16[128,4,8,128]{0,3,2,1:T(8,128)(2,1)S(1)} %fusion.23, bf16[128,4,128]{0,2,1:T(8,128)(2,1)S(1)} %get-tuple-element.143), kind=kOutput, calls=%fused_computation.37 | convolution fusion | flops 134742016 | bytes 3276800 | tf_op jit(solution)/shard_map/cond/branch_1_fun/tgru,uge->tgre/dot_general | solution.py:143
  47.8 3.0 %copy.164 = f32[128,4,8,128]{0,3,2,1:T(8,128)} copy(f32[128,4,8,128]{3,0,2,1:T(8,128)} %multiply_bitcast_fusion.1) | data formatting | bytes 4194304 | tf_op jit(solution)/shard_map/cond | solution.py:161
  50.8 10.0 %conditional.6 = (f32[128,4,128]{2,0,1:T(8,128)}, f32[128,4,128]{2,0,1:T(8,128)}, f32[128,4,8,128]{0,3,2,1:T(8,128)}) conditional(s32[]{:T(128)} %bitcast.35, () %tuple.44, (pred[128,128]{0,1:T(8,128)(4,1)}, bf16[128,4,128]{0,2,1:T(8,128)(2,1)S(1)}, bf16[128,4,8,128]{0,3,2,1:T(8,128)(2,1)S(1)}, f32[128,4,8]{0,2,1:T(8,128)}, ...), branch_computations={%region_11.12_spmd, %region_12.13_spmd} | conditional | flops 675348480 | bytes 20889624 | solution.py:161
  57.8 3.0 %copy.162 = f32[128,4,8,128]{0,3,2,1:T(8,128)} copy(f32[128,4,8,128]{3,0,2,1:T(8,128)} %multiply_bitcast_fusion) | data formatting | bytes 4194304 | tf_op jit(solution)/shard_map/cond | solution.py:161
  60.8 3.4 %fusion.35 = f32[128,4,8,128]{0,3,2,1:T(8,128)S(1)} fusion(f32[128,4,8,128]{0,3,2,1:T(8,128)} %get-tuple-element.153, f32[128,4,8,128]{0,3,2,1:T(8,128)} %get-tuple-element.152, f32[4,128,128,8]{2,1,3,0:T(8,128)} %fusion.57), kind=kLoop, calls=%fused_computation.54 | loop fusion | flops 1572864 | bytes 8388608 | tf_op jit(solution)/shard_map/add | solution.py:168
  67.3 2.9 %copy.160 = f32[1,128,4096]{2,1,0:T(8,128)} copy(f32[1,128,4096]{1,2,0:T(8,128)} %bitcast.227) | data formatting | bytes 4194304 | tf_op jit(solution)/shard_map/concatenate | solution.py:62
  70.3 3.0 %copy.106 = f32[1,128,4096]{2,1,0:T(8,128)} copy(f32[1,128,4096]{1,2,0:T(8,128)} %bitcast.226) | data formatting | bytes 4194304 | tf_op jit(solution)/shard_map/reshape | solution.py:181
  78.8 3.4 %collective-permute-start.6 = (f32[128,4,128]{0,2,1:T(8,128)}, f32[128,4,128]{0,2,1:T(8,128)}, u32[]{:S(2)}, u32[]{:S(2)}) collective-permute-start(f32[128,4,128]{0,2,1:T(8,128)} %copy.110), channel_id=1, source_target_pairs={{8,0},{12,4},{16,8},{20,12},{24,16},{28,20},{9,1},{13,5},{17,9},{2... | collective-permute-start | bytes 786440 | tf_op jit(solution)/shard_map/ppermute | solution.py:23
  82.1 4.2 %add_convert_fusion = bf16[1,128,4096]{2,1,0:T(8,128)(2,1)} fusion(f32[1,128,4096]{2,1,0:T(8,128)} %copy.160, f32[1,128,4096]{2,1,0:T(8,128)} %copy.106, f32[1,128,4096]{2,1,0:T(8,128)} %mul.242), kind=kLoop, calls=%fused_computation.67 | loop fusion | flops 1572864 | bytes 7340032 | tf_op jit(solution)/shard_map/convert_element_type | solution.py:182
  86.3 4.7 %collective-permute-start.4 = (bf16[1,128,4096]{2,1,0:T(8,128)(2,1)}, bf16[1,128,4096]{2,1,0:T(8,128)(2,1)}, u32[]{:S(2)}, u32[]{:S(2)}) collective-permute-start(bf16[1,128,4096]{2,1,0:T(8,128)(2,1)} %add_convert_fusion), channel_id=1, source_target_pairs={{1,0},{2,1},{3,2},{5,4},{6,5},{7,6},{9,8},{10,9},{11,10},{13,12},{... | collective-permute-start | bytes 3145736 | tf_op jit(solution)/shard_map/ppermute | solution.py:23
  92.8 3.1 %collective-permute-start.7 = (f32[128,4,128]{0,2,1:T(8,128)}, f32[128,4,128]{0,2,1:T(8,128)}, u32[]{:S(2)}, u32[]{:S(2)}) collective-permute-start(f32[128,4,128]{0,2,1:T(8,128)} %copy.112), channel_id=1, source_target_pairs={{4,0},{8,4},{12,8},{16,12},{20,16},{24,20},{28,24},{5,1},{9,5},{13... | collective-permute-start | bytes 786440 | tf_op jit(solution)/shard_map/ppermute | solution.py:23
  97.6 2.0 %collective-permute-start.8 = (f32[128,4,128]{0,2,1:T(8,128)}, f32[128,4,128]{0,2,1:T(8,128)}, u32[]{:S(2)}, u32[]{:S(2)}) collective-permute-start(f32[128,4,128]{0,2,1:T(8,128)} %copy.113), channel_id=1, source_target_pairs={{8,0},{12,4},{16,8},{20,12},{24,16},{28,20},{9,1},{13,5},{17,9},{2... | collective-permute-start | bytes 786440 | tf_op jit(solution)/shard_map/ppermute | solution.py:23
  102.9 6.6 %collective-permute-done.8 = f32[128,4,128]{0,2,1:T(8,128)} collective-permute-done((f32[128,4,128]{0,2,1:T(8,128)}, f32[128,4,128]{0,2,1:T(8,128)}, u32[]{:S(2)}, u32[]{:S(2)}) %collective-permute-start.8) | collective-permute-done | bytes 262176 | tf_op jit(solution)/shard_map/ppermute | solution.py:23
  109.6 2.2 %add_convert_fusion.1 = bf16[128,4,128]{0,2,1:T(8,128)(2,1)S(1)} fusion(f32[128,4,128]{0,2,1:T(8,128)} %collective-permute-done.7, f32[128,4,128]{0,2,1:T(8,128)} %collective-permute-done.8, bf16[128,4,8,128]{0,3,2,1:T(8,128)(2,1)S(1)} %bitcast.223, f32[4,128,128,8]{2,1,3,0:T(8,128)} %copy-done, f32[128,4,8]{0,2,1:T(8,128)} %copy-done.9, ...), kind=kOutput, calls=%fused_computation.84 | convolution fusion | flops 136511488 | bytes 3833856 | tf_op jit(solution)/shard_map/tgru,tgre->uge/dot_general | solution.py:150
  112.6 2.3 %copy.186 = bf16[1,128,4096]{2,1,0:T(8,128)(2,1)} copy(bf16[1,128,4096]{2,1,0:T(8,128)(2,1)} %collective-permute-done.4) | data formatting | bytes 2097152
  (88 shorter events, 50.9 us)
Async XLA Ops:
  0.6 15.4 %copy-start.14 = (s32[1,2]{1,0:T(1,128)S(1)}, s32[1,2]{1,0:T(1,128)}, u32[]{:S(2)}) copy-start(s32[1,2]{1,0:T(1,128)} %param.21) | copy-start | bytes 28
  0.6 16.7 %copy-start.4 = (bf16[1,128,4096]{2,1,0:T(8,128)(2,1)S(1)}, bf16[1,128,4096]{2,1,0:T(8,128)(2,1)}, u32[]{:S(2)}) copy-start(bf16[1,128,4096]{2,1,0:T(8,128)(2,1)} %param.15) | copy-start | bytes 3145732
  3.5 27.6 %collective-permute-start.1 = (bf16[128,4,128]{0,2,1:T(8,128)(2,1)}, bf16[128,4,128]{0,2,1:T(8,128)(2,1)S(1)}, u32[]{:S(2)}, u32[]{:S(2)}) collective-permute-start(bf16[128,4,128]{0,2,1:T(8,128)(2,1)} %fusion.53), channel_id=1, source_target_pairs={{0,8},{4,12},{8,16},{12,20},{16,24},{20,28},{1,9},{5,13},{9,17},{1... | collective-permute-start | bytes 393224 | tf_op jit(solution)/shard_map/ppermute | solution.py:23
  6.7 26.7 %collective-permute-start = (bf16[128,4,128]{0,2,1:T(8,128)(2,1)}, bf16[128,4,128]{0,2,1:T(8,128)(2,1)S(1)}, u32[]{:S(2)}, u32[]{:S(2)}) collective-permute-start(bf16[128,4,128]{0,2,1:T(8,128)(2,1)} %fusion.53), channel_id=1, source_target_pairs={{0,4},{4,8},{8,12},{12,16},{16,20},{20,24},{24,28},{1,5},{5,9},{9,... | collective-permute-start | bytes 393224 | tf_op jit(solution)/shard_map/ppermute | solution.py:23
  11.5 30.1 %collective-permute-start.3 = (bf16[128,4,128]{0,2,1:T(8,128)(2,1)}, bf16[128,4,128]{0,2,1:T(8,128)(2,1)}, u32[]{:S(2)}, u32[]{:S(2)}) collective-permute-start(bf16[128,4,128]{0,2,1:T(8,128)(2,1)} %bitcast.37), channel_id=1, source_target_pairs={{0,8},{4,12},{8,16},{12,20},{16,24},{20,28},{1,9},{5,13},{9,17},{1... | collective-permute-start | bytes 393224 | tf_op jit(solution)/shard_map/ppermute | solution.py:23
  13.4 37.4 %collective-permute-start.2 = (bf16[128,4,128]{0,2,1:T(8,128)(2,1)}, bf16[128,4,128]{0,2,1:T(8,128)(2,1)}, u32[]{:S(2)}, u32[]{:S(2)}) collective-permute-start(bf16[128,4,128]{0,2,1:T(8,128)(2,1)} %bitcast.37), channel_id=1, source_target_pairs={{0,4},{4,8},{8,12},{12,16},{16,20},{20,24},{24,28},{1,5},{5,9},{9,... | collective-permute-start | bytes 393224 | tf_op jit(solution)/shard_map/ppermute | solution.py:23
  18.1 2.0 %copy-start.1 = (f32[1,128,4096]{1,2,0:T(8,128)}, f32[1,128,4096]{1,2,0:T(8,128)S(1)}, u32[]{:S(2)}) copy-start(f32[1,128,4096]{1,2,0:T(8,128)S(1)} %convert_element_type.119) | copy-start | bytes 6291460
  18.1 2.7 %copy-start.5 = (bf16[1,128,4096]{2,1,0:T(8,128)(2,1)S(1)}, bf16[1,128,4096]{2,1,0:T(8,128)(2,1)}, u32[]{:S(2)}) copy-start(bf16[1,128,4096]{2,1,0:T(8,128)(2,1)} %param.19) | copy-start | bytes 3145732
  20.1 1.4 %copy-start.6 = (bf16[1,128,4096]{2,1,0:T(8,128)(2,1)S(1)}, bf16[1,128,4096]{2,1,0:T(8,128)(2,1)}, u32[]{:S(2)}) copy-start(bf16[1,128,4096]{2,1,0:T(8,128)(2,1)} %param.18) | copy-start | bytes 3145732
  23.9 1.5 %copy-start.13 = (s32[128]{0:T(128)S(1)}, s32[128]{0:T(128)}, u32[]{:S(2)}) copy-start(s32[128]{0:T(128)} %param.20) | copy-start | bytes 1540
  25.5 4.2 %copy-start.7 = (pred[128,128]{0,1:T(8,128)(4,1)}, pred[128,128]{0,1:T(8,128)(4,1)S(1)}, u32[]{:S(2)}) copy-start(pred[128,128]{0,1:T(8,128)(4,1)S(1)} %get-tuple-element.168) | copy-start | bytes 49156
  25.5 5.6 %copy-start.11 = (pred[128,128]{0,1:T(8,128)(4,1)}, pred[128,128]{0,1:T(8,128)(4,1)S(1)}, u32[]{:S(2)}) copy-start(pred[128,128]{0,1:T(8,128)(4,1)S(1)} %get-tuple-element.170) | copy-start | bytes 49156
  25.6 7.9 %copy-start.10 = (pred[128,128]{0,1:T(8,128)(4,1)}, pred[128,128]{0,1:T(8,128)(4,1)S(1)}, u32[]{:S(2)}) copy-start(pred[128,128]{0,1:T(8,128)(4,1)S(1)} %get-tuple-element.169) | copy-start | bytes 49156
  28.2 2.0 %copy-start.3 = (bf16[1,128,4096]{1,2,0:T(8,128)(2,1)S(1)}, bf16[1,128,4096]{1,2,0:T(8,128)(2,1)}, u32[]{:S(2)}) copy-start(bf16[1,128,4096]{1,2,0:T(8,128)(2,1)} %copy.93) | copy-start | bytes 3145732
  29.7 1.3 %copy-start = (f32[4,128,128,8]{2,1,3,0:T(8,128)}, f32[4,128,128,8]{2,1,3,0:T(8,128)S(1)}, u32[]{:S(2)}) copy-start(f32[4,128,128,8]{2,1,3,0:T(8,128)S(1)} %get-tuple-element.174) | copy-start | bytes 6291460
  36.5 5.0 %copy-start.9 = (f32[128,4,8]{0,2,1:T(8,128)}, f32[128,4,8]{0,2,1:T(8,128)S(1)}, u32[]{:S(2)}) copy-start(f32[128,4,8]{0,2,1:T(8,128)S(1)} %log_add_fusion) | copy-start | bytes 49156
  38.9 2.7 %copy-start.12 = (pred[128,128]{0,1:T(8,128)(4,1)S(1)}, pred[128,128]{0,1:T(8,128)(4,1)}, u32[]{:S(2)}) copy-start(pred[128,128]{0,1:T(8,128)(4,1)} %copy-done.11) | copy-start | bytes 49156
  64.2 1.4 %copy-start.2 = (f32[128,4,8,128]{0,3,2,1:T(8,128)}, f32[128,4,8,128]{0,3,2,1:T(8,128)S(1)}, u32[]{:S(2)}) copy-start(f32[128,4,8,128]{0,3,2,1:T(8,128)S(1)} %fusion.35) | copy-start | bytes 6291460
  75.0 24.7 %collective-permute-start.5 = (f32[128,4,128]{0,2,1:T(8,128)}, f32[128,4,128]{0,2,1:T(8,128)S(1)}, u32[]{:S(2)}, u32[]{:S(2)}) collective-permute-start(f32[128,4,128]{0,2,1:T(8,128)} %copy.109), channel_id=1, source_target_pairs={{4,0},{8,4},{12,8},{16,12},{20,16},{24,20},{28,24},{5,1},{9,5},{13... | collective-permute-start | bytes 786440 | tf_op jit(solution)/shard_map/ppermute | solution.py:23
  78.8 20.9 %collective-permute-start.6 = (f32[128,4,128]{0,2,1:T(8,128)}, f32[128,4,128]{0,2,1:T(8,128)}, u32[]{:S(2)}, u32[]{:S(2)}) collective-permute-start(f32[128,4,128]{0,2,1:T(8,128)} %copy.110), channel_id=1, source_target_pairs={{8,0},{12,4},{16,8},{20,12},{24,16},{28,20},{9,1},{13,5},{17,9},{2... | collective-permute-start | bytes 786440 | tf_op jit(solution)/shard_map/ppermute | solution.py:23
  86.3 26.3 %collective-permute-start.4 = (bf16[1,128,4096]{2,1,0:T(8,128)(2,1)}, bf16[1,128,4096]{2,1,0:T(8,128)(2,1)}, u32[]{:S(2)}, u32[]{:S(2)}) collective-permute-start(bf16[1,128,4096]{2,1,0:T(8,128)(2,1)} %add_convert_fusion), channel_id=1, source_target_pairs={{1,0},{2,1},{3,2},{5,4},{6,5},{7,6},{9,8},{10,9},{11,10},{13,12},{... | collective-permute-start | bytes 3145736 | tf_op jit(solution)/shard_map/ppermute | solution.py:23
  92.8 10.2 %collective-permute-start.7 = (f32[128,4,128]{0,2,1:T(8,128)}, f32[128,4,128]{0,2,1:T(8,128)}, u32[]{:S(2)}, u32[]{:S(2)}) collective-permute-start(f32[128,4,128]{0,2,1:T(8,128)} %copy.112), channel_id=1, source_target_pairs={{4,0},{8,4},{12,8},{16,12},{20,16},{24,20},{28,24},{5,1},{9,5},{13... | collective-permute-start | bytes 786440 | tf_op jit(solution)/shard_map/ppermute | solution.py:23
  97.6 11.9 %copy-start.8 = (pred[128,128]{0,1:T(8,128)(4,1)S(1)}, pred[128,128]{0,1:T(8,128)(4,1)}, u32[]{:S(2)}) copy-start(pred[128,128]{0,1:T(8,128)(4,1)} %copy-done.7) | copy-start | bytes 49156
  97.6 11.9 %collective-permute-start.8 = (f32[128,4,128]{0,2,1:T(8,128)}, f32[128,4,128]{0,2,1:T(8,128)}, u32[]{:S(2)}, u32[]{:S(2)}) collective-permute-start(f32[128,4,128]{0,2,1:T(8,128)} %copy.113), channel_id=1, source_target_pairs={{8,0},{12,4},{16,8},{20,12},{24,16},{28,20},{9,1},{13,5},{17,9},{2... | collective-permute-start | bytes 786440 | tf_op jit(solution)/shard_map/ppermute | solution.py:23
where the time goes:
time: 116 us; the launch traced here: 115 us
  local copies, waits for them, and re-layouts  34.2 us (29%)
  matrix products  25.6 us (22%)
  starting transfers between devices  25.2 us (22%)
  other arithmetic  20.7 us (18%)
  waiting for transfers between devices  6.63 us (6%)
  between operations  2.41 us (2%)
    ppermute x9, starting transfers between devices, from_behind(): lax.ppermute(value, axis, [(source, source + steps) for source in range(i...  25.2 us
    cond x6, local copies, waits for them, and re-layouts, shards(): lax.cond(listed[distance - 1] == 1, lambda k_blk=blocks[distance][0], v_b...  13.1 us
    unnamed x37, local copies, waits for them, and re-layouts  10.3 us
    ppermute x9, waiting for transfers between devices, from_behind(): lax.ppermute(value, axis, [(source, source + steps) for source in range(i...  6.63 us
    dot_general x3, matrix products, tile_grads(): jnp.einsum('tgru,uge->tgre', dscore, k_blk, preferred_element_type=jnp.fl...  6.48 us
    dot_general x3, matrix products, tile_grads(): jnp.einsum('tgre,uge->tgru', grad_rows, v_blk, preferred_element_type=jnp...  5.16 us
    dot_general x3, matrix products, tile_grads(): jnp.einsum('tgru,tgre->uge', prob_b, grad_rows, preferred_element_type=jn...  4.58 us
    convert_element_type x1, other arithmetic, shards(): query_grad = undo_rope(dq_sum.reshape(tok_rows, HQ, HD), cosine, sine_tab...  4.17 us
  transfers between devices with their start and end apart: 9, of which 1 were waited for; matrix products, arithmetic and copies ran while one was open for 44% of the time, Pallas kernels for 0%

commit v1 on v0

v1 whole, which is shorter than its diff:
```python
import math

import jax
import jax.numpy as jnp
from jax import lax
from jax.experimental import pallas as pl
from jax.experimental.pallas import tpu as pltpu
from jax.sharding import PartitionSpec as P

HQ = 32
HK = 4
HD = 128
RATIO = HQ // HK
HALF = HD // 2
FETCH = 2
PAIR = 2

ROPE_BASE = 1000000.0
TRAINED_CONTEXT = 32768.0
YARN_FACTOR = 4.0
NEG_LARGE = -1e30
SCORE_SCALE = HD ** (-0.5)
EXP2_SCALE = SCORE_SCALE / math.log(2.0)

F32 = jnp.float32
BF16 = jnp.bfloat16


def from_behind(value, axis, steps):
    count = lax.axis_size(axis)
    initial, last = (max(0, -steps), min(count, count - steps))
    return lax.ppermute(value, axis, [(source, source + steps) for source in range(initial, last)])


def dot_nn(left, right):
    return lax.dot_general(left, right, (((1,), (0,)), ((), ())), preferred_element_type=F32)


def dot_nt(left, right):
    return lax.dot_general(left, right, (((1,), (1,)), ((), ())), preferred_element_type=F32)


def frequencies(rows, columns):
    def correction(rotations):
        return HD * math.log(TRAINED_CONTEXT / (rotations * 2.0 * math.pi)) / (2.0 * math.log(ROPE_BASE))

    lower_dim = max(math.floor(correction(32.0)), 0)
    upper_dim = min(math.ceil(correction(1.0)), HD - 1)
    spread_dims = max(upper_dim - lower_dim, 0.001)
    indices = lax.broadcasted_iota(jnp.int32, (rows, columns), 0).astype(F32)
    extrapolated = jnp.exp(indices * F32(-2.0 / HD * math.log(ROPE_BASE)))
    ramp_weight = jnp.clip((indices - lower_dim) / spread_dims, 0.0, 1.0)
    return extrapolated / YARN_FACTOR * ramp_weight + extrapolated * (1.0 - ramp_weight)


def half_tables(positions):
    factor = 0.1 * math.log(YARN_FACTOR) + 1.0
    angles = frequencies(HALF, positions.shape[1]) * positions.astype(F32)
    return jnp.cos(angles) * factor, jnp.sin(angles) * factor


def upright(cos_t, sin_t):
    cosine = jnp.concatenate([cos_t, cos_t], axis=0).T
    signed_sine = jnp.concatenate([sin_t, -sin_t], axis=0).T
    return cosine, signed_sine


def rotate(values, cosine, signed_sine):
    return values * cosine - pltpu.roll(values, HALF, 1) * signed_sine


def unrotate(values, cosine, signed_sine):
    return values * cosine + pltpu.roll(values, HALF, 1) * signed_sine


def head_columns(head):
    return slice(head * HD, (head + 1) * HD)


def stack_heads(ref, group, first):
    return jnp.concatenate([ref[group, :, head_columns(first + i)] for i in range(PAIR)], axis=0)


def block_diagonal(upper, lower):
    zero = jnp.zeros_like(upper)
    return jnp.concatenate(
        [jnp.concatenate([upper, zero], axis=1), jnp.concatenate([zero, lower], axis=1)], axis=0
    )


def group_rows(ref, group, columns):
    pairs = range(RATIO // PAIR)
    return jnp.concatenate([ref[group * len(pairs) + i, :, columns] for i in pairs], axis=0)


def pack_kernel(k_hbm, v_hbm, kv_ref, arrived):
    copies = [
        pltpu.make_async_copy(source.at[:, head_columns(group)], kv_ref.at[which, group], arrived.at[which, group])
        for which, source in enumerate((k_hbm, v_hbm))
        for group in range(HK)
    ]
    for copy in copies:
        copy.start()
    for copy in copies:
        copy.wait()


def own_kernel(
    first_ref, doc_ref, q_hbm, k_hbm, v_hbm, o_hbm, g_hbm,
    qg_ref, prob_ref, ds_ref, kt_ref, stat_ref, half_ref, cos_ref, sin_ref, cos12_ref, sin12_ref,
    q_ref, k_ref, v_ref, o_ref, g_ref, arrived,
):
    rows = q_hbm.shape[0]
    arguments = ((k_hbm, k_ref), (q_hbm, q_ref), (v_hbm, v_ref), (g_hbm, g_ref), (o_hbm, o_ref))

    def fetch(which, group):
        source, buffer = arguments[which]
        width = buffer.shape[2]
        columns = pl.ds(pl.multiple_of(group * width, width), width)
        return pltpu.make_async_copy(source.at[:, columns], buffer.at[group], arrived.at[which, group])

    for group in range(HK):
        for which in range(len(arguments)):
            fetch(which, group).start()

    doc_row = doc_ref[...] - first_ref[0]
    columns = lax.broadcasted_iota(jnp.int32, (1, rows), 1)
    cos_t, sin_t = half_tables(columns - doc_row)
    half_ref[0] = cos_t * SCORE_SCALE
    half_ref[1] = sin_t * SCORE_SCALE
    cos_ref[...], sin_ref[...] = upright(cos_t, sin_t)
    reach = doc_row[:, 0:1]
    for distance in range(FETCH, 0, -1):
        at = slice((FETCH - distance) * rows, (FETCH - distance + 1) * rows)
        back_cos, back_sin = upright(*half_tables(columns - distance * rows - reach))
        cos12_ref[at, :] = back_cos
        sin12_ref[at, :] = back_sin
    key_idx = lax.broadcasted_iota(jnp.int32, (rows, rows), 0)
    query_idx = lax.broadcasted_iota(jnp.int32, (rows, rows), 1)
    mask = (key_idx <= query_idx) & (key_idx >= doc_row)
    bias = jnp.where(mask, 0.0, NEG_LARGE)
    bias = jnp.concatenate([bias] * PAIR, axis=1)
    ones = jnp.ones((8, HD), BF16)

    @pl.loop(0, HK)
    def _(group):
        for which in range(len(arguments)):
            fetch(which, group).wait()
        cosine = cos_ref[...]
        signed_sine = sin_ref[...]
        k_rot = rotate(k_ref[group].astype(F32), cosine, signed_sine)
        kt_ref[group] = k_rot.T.astype(BF16)
        left = block_diagonal(k_rot.astype(BF16), v_ref[group])

        def products(first):
            pair = group * (RATIO // PAIR) + first // PAIR
            for i in range(PAIR):
                rows_of = slice(i * rows, (i + 1) * rows)
                q_rot = rotate(q_ref[group, :, head_columns(first + i)].astype(F32), cosine, signed_sine)
                qg_ref[pair, rows_of, :HD] = q_rot.astype(BF16)
            grads = stack_heads(g_ref, group, first)
            qg_ref[pair, :, HD:] = grads
            product = grads.astype(F32) * stack_heads(o_ref, group, first).astype(F32)
            high = product.astype(BF16)
            low = (product - high.astype(F32)).astype(BF16)
            delta = (dot_nt(ones, high) + dot_nt(ones, low))[0:1]
            both = dot_nt(left, qg_ref[pair])
            return both[:rows], both[rows:], delta

        def finish(first, scores, dprob, delta):
            at = slice(first * HD, (first + PAIR) * HD)
            scores = scores + bias
            largest = jnp.max(scores, axis=0, keepdims=True)
            prob = jnp.exp2((scores - largest) * EXP2_SCALE)
            total = jnp.sum(prob, axis=0, keepdims=True)
            dscore = (prob * (dprob - delta)).astype(BF16)
            prob_ref[group, :, at] = prob.astype(BF16)
            ds_ref[group, :, at] = dscore
            stat_ref[group, 0:1, at] = largest
            stat_ref[group, 1:2, at] = total
            stat_ref[group, 2:3, at] = delta

        ahead = products(0)
        for first in range(0, RATIO, PAIR):
            now = ahead
            if first + PAIR < RATIO:
                ahead = products(first + PAIR)
            finish(first, *now)


def cross_kernel(
    first_ref, list_ref, doc_ref, qg_ref, kv2_ref, kv1_ref, ds0_ref, kt_ref, stat_ref, half_ref, cos12_ref, sin12_ref,
    dq_ref, ret2_ref, ret1_ref, scale_ref, own_ref, prob_buf, ds_buf,
):
    rows = doc_ref.shape[1]
    doc_row = doc_ref[...] - first_ref[0]
    reach = doc_row[:, 0:1]
    in_reach = jnp.where(doc_row == reach, 1.0, 0.0)
    in_reach = jnp.concatenate([in_reach] * PAIR, axis=1)
    key_idx = lax.broadcasted_iota(jnp.int32, (rows, PAIR * rows), 0)
    far = jnp.where(list_ref[0, 1] == 1, -2 * rows, -(1 << 30))
    near = jnp.where(list_ref[0, 0] == 1, -rows, -(1 << 30))
    bias = jnp.concatenate([key_idx + far, key_idx + near], axis=0)
    bias = jnp.where(bias >= reach, 0.0, NEG_LARGE)

    def attend(skipped):
        used = FETCH * rows - skipped
        behind_by_two = rows - skipped
        own_bias = bias[skipped:]

        def key_rows(which, group):
            near_rows = kv1_ref[which, group]
            if behind_by_two == 0:
                return near_rows
            return jnp.concatenate([kv2_ref[which, group, skipped:, :], near_rows], axis=0)

        @pl.loop(0, HK)
        def _(group):
            k_rot = rotate(key_rows(0, group).astype(F32), cos12_ref[skipped:, :], sin12_ref[skipped:, :])
            k_rot_t = jnp.concatenate([k_rot.T.astype(BF16), kt_ref[group]], axis=1)
            left = block_diagonal(k_rot.astype(BF16), key_rows(1, group))
            cos_t = jnp.concatenate([half_ref[0]] * PAIR, axis=1)
            sin_t = jnp.concatenate([half_ref[1]] * PAIR, axis=1)

            def products(first):
                both = dot_nt(left, qg_ref[group * (RATIO // PAIR) + first // PAIR])
                return both[:used], both[used:]

            def middle(first, scores, dprob):
                at = slice(first * HD, (first + PAIR) * HD)
                own_max = stat_ref[group, 0:1, at]
                own_sum = stat_ref[group, 1:2, at]
                delta = stat_ref[group, 2:3, at]
                scores = scores + own_bias
                largest = jnp.maximum(own_max, jnp.max(scores, axis=0, keepdims=True))
                prob = jnp.exp2((scores - largest) * EXP2_SCALE)
                total = jnp.sum(prob, axis=0, keepdims=True) * in_reach
                own_scale = jnp.exp2(jnp.where(in_reach > 0.0, own_max - largest, 0.0) * EXP2_SCALE)
                inverse = 1.0 / (own_sum * own_scale + total)
                own_scale = own_scale * inverse
                scale_ref[group, 0:1, at] = own_scale
                prob = (prob * (inverse * in_reach)).astype(BF16)
                dscore = prob * (dprob - delta).astype(BF16)
                prob_buf[:used, at] = prob
                ds_buf[:used, at] = dscore
                own_dscore = ds0_ref[group, :, at] * own_scale.astype(BF16)
                own_ref[group, :, at] = own_dscore
                return jnp.concatenate([dscore, own_dscore], axis=0)

            def finish(first, dscore):
                dq = dot_nn(k_rot_t, dscore)
                upper, lower = dq[:HALF], dq[HALF:]
                dq = jnp.concatenate([upper * cos_t + lower * sin_t, lower * cos_t - upper * sin_t], axis=0)
                dq = dq.astype(BF16)
                for i in range(PAIR):
                    lanes = pl.ds(pl.multiple_of((group * RATIO + first + i) * HD, HD), HD)
                    dq_ref[0, :, lanes] = dq[:, head_columns(i)].T

            ahead = products(0)
            behind = None
            for first in range(0, RATIO, PAIR):
                now = ahead
                if first + PAIR < RATIO:
                    ahead = products(first + PAIR)
                done = middle(first, *now)
                if behind is not None:
                    finish(first - PAIR, behind)
                behind = done
            finish(RATIO - PAIR, behind)
            dk = dot_nn(ds_buf[:used, :], group_rows(qg_ref, group, slice(HD))) * SCORE_SCALE
            dv = dot_nn(prob_buf[:used, :], group_rows(qg_ref, group, slice(HD, 2 * HD)))
            for which, grad in enumerate((dk.astype(BF16), dv.astype(BF16))):
                ret1_ref[which, group] = grad[behind_by_two:]
                if skipped:
                    ret2_ref[which, group, :skipped, :] = jnp.zeros((skipped, HD), BF16)
                if behind_by_two:
                    ret2_ref[which, group, skipped:, :] = grad[:behind_by_two]

    farthest = jnp.min(doc_row.astype(F32))
    pl.when(farthest >= -rows)(lambda: attend(rows))
    pl.when((farthest < -rows) & (farthest >= -rows - rows // 2))(lambda: attend(rows // 2))
    pl.when(farthest < -rows - rows // 2)(lambda: attend(0))


def own_kv_kernel(qg_ref, prob_ref, ds_ref, scale_ref, dk_ref, dv_ref):
    @pl.loop(0, HK)
    def _(group):
        prob = (prob_ref[group].astype(F32) * scale_ref[group, 0:1, :]).astype(BF16)
        dk_ref[group] = dot_nn(ds_ref[group], group_rows(qg_ref, group, slice(HD))) * SCORE_SCALE
        dv_ref[group] = dot_nn(prob, group_rows(qg_ref, group, slice(HD, 2 * HD)))


def sum_kernel(
    dk_ref, dv_ref, ret2_ref, ret1_ref, cos_ref, sin_ref, dq_ref, key_hbm, value_hbm, handed_hbm, key_buf, value_buf, copied
):
    rows = dq_ref.shape[1]
    half = rows // 2
    copies = [
        pltpu.make_async_copy(dq_ref.at[:, pl.ds(i * half, half)], handed_hbm.at[:, pl.ds(i * half, half)], copied.at[i])
        for i in range(2)
    ]
    for copy in copies:
        copy.start()
    for group in range(HK):
        at = head_columns(group)
        dv = dv_ref[group] + ret1_ref[1, group].astype(F32) + ret2_ref[1, group].astype(F32)
        value_buf[0, :, at] = dv.astype(BF16)
    copies.append(pltpu.make_async_copy(value_buf, value_hbm, copied.at[2]))
    copies[-1].start()
    for group in range(HK):
        at = head_columns(group)
        dk = dk_ref[group] + ret1_ref[0, group].astype(F32) + ret2_ref[0, group].astype(F32)
        key_buf[0, :, at] = unrotate(dk, cos_ref[...], sin_ref[...]).astype(BF16)
    copies.append(pltpu.make_async_copy(key_buf, key_hbm, copied.at[3]))
    copies[-1].start()
    for copy in copies:
        copy.wait()


def cost(flops, moved, exps=0):
    return pl.CostEstimate(flops=int(flops), bytes_accessed=int(moved), transcendentals=int(exps))


def shards(query_heads, key_heads, value_heads, attn_output, output_grad, doc_start, fetch_list):
    rows = query_heads.shape[1]
    wide = RATIO * HD
    kv_width = HK * HD
    first_row = (lax.axis_index("ctx") * rows).astype(jnp.int32).reshape(1)
    doc_row = doc_start.reshape(1, rows)
    smem = pl.BlockSpec(memory_space=pltpu.SMEM)
    vmem = pl.BlockSpec(memory_space=pltpu.VMEM)
    hbm = pl.BlockSpec(memory_space=pltpu.HBM)
    params = pltpu.CompilerParams(vmem_limit_bytes=40 * 1024 * 1024)
    shape = jax.ShapeDtypeStruct
    block_flops = 2 * HQ * rows * rows * HD
    arguments = [
        pltpu.with_memory_space_constraint(x[0], pltpu.HBM)
        for x in (query_heads, key_heads, value_heads, attn_output, output_grad)
    ]

    kv = pl.pallas_call(
        pack_kernel,
        in_specs=[hbm, hbm],
        out_specs=vmem,
        out_shape=shape((2, HK, rows, HD), BF16),
        scratch_shapes=[pltpu.SemaphoreType.DMA((2, HK))],
        compiler_params=params,
        cost_estimate=cost(0, 2**19),
        name="pack_keys",
    )(arguments[1], arguments[2])
    kv2 = from_behind(kv, "ctx", 2)
    kv1 = from_behind(kv, "ctx", 1)

    qg, prob0, ds0, k_own_t, stat, half, cos, sin, cos12, sin12 = pl.pallas_call(
        own_kernel,
        in_specs=[smem, vmem] + [hbm] * 5,
        out_specs=[vmem] * 10,
        out_shape=[
            shape((HQ // PAIR, PAIR * rows, 2 * HD), BF16),
            shape((HK, rows, RATIO * rows), BF16),
            shape((HK, rows, RATIO * rows), BF16),
            shape((HK, HD, rows), BF16),
            shape((HK, 8, RATIO * rows), F32),
            shape((2, HALF, rows), F32),
            shape((rows, HD), F32),
            shape((rows, HD), F32),
            shape((FETCH * rows, HD), F32),
            shape((FETCH * rows, HD), F32),
        ],
        scratch_shapes=[
            pltpu.VMEM((HK, rows, wide), BF16),
            pltpu.VMEM((HK, rows, HD), BF16),
            pltpu.VMEM((HK, rows, HD), BF16),
            pltpu.VMEM((HK, rows, wide), BF16),
            pltpu.VMEM((HK, rows, wide), BF16),
            pltpu.SemaphoreType.DMA((5, HK)),
        ],
        compiler_params=params,
        cost_estimate=cost(3 * block_flops, 9 * 2**20, HQ * rows * rows),
        name="own_block",
    )(first_row, pltpu.with_memory_space_constraint(doc_row, pltpu.HBM), *arguments)

    dq, ret2, ret1, scale, ds_own = pl.pallas_call(
        cross_kernel,
        in_specs=[smem, smem] + [vmem] * 10,
        out_specs=[vmem] * 5,
        out_shape=[
            shape((1, rows, HQ * HD), BF16),
            shape((2, HK, rows, HD), BF16),
            shape((2, HK, rows, HD), BF16),
            shape((HK, 8, RATIO * rows), F32),
            shape((HK, rows, RATIO * rows), BF16),
        ],
        scratch_shapes=[
            pltpu.VMEM((FETCH * rows, RATIO * rows), BF16),
            pltpu.VMEM((FETCH * rows, RATIO * rows), BF16),
        ],
        compiler_params=params,
        cost_estimate=cost(10 * block_flops, 6 * 2**20, 2 * HQ * rows * rows),
        name="cross_blocks",
    )(first_row, fetch_list, doc_row, qg, kv2, kv1, ds0, k_own_t, stat, half, cos12, sin12)

    arrived1 = from_behind(ret1, "ctx", -1)
    arrived2 = from_behind(ret2, "ctx", -2)
    dq_next = from_behind(dq, "section", -1)

    dk0, dv0 = pl.pallas_call(
        own_kv_kernel,
        in_specs=[vmem] * 4,
        out_specs=[vmem] * 2,
        out_shape=[shape((HK, rows, HD), F32), shape((HK, rows, HD), F32)],
        compiler_params=params,
        cost_estimate=cost(2 * block_flops, 5 * 2**20),
        name="own_keys",
    )(qg, prob0, ds_own, scale)

    key_grad, value_grad, handed_grad = pl.pallas_call(
        sum_kernel,
        in_specs=[vmem] * 6 + [pl.BlockSpec(memory_space=pl.ANY)],
        out_specs=[hbm] * 3,
        out_shape=[
            shape((1, rows, kv_width), BF16),
            shape((1, rows, kv_width), BF16),
            shape((1, rows, HQ * HD), BF16),
        ],
        scratch_shapes=[
            pltpu.VMEM((1, rows, kv_width), BF16),
            pltpu.VMEM((1, rows, kv_width), BF16),
            pltpu.SemaphoreType.DMA((4,)),
        ],
        compiler_params=params,
        cost_estimate=cost(0, 3 * 2**20),
        name="sum_keys",
    )(dk0, dv0, arrived2, arrived1, cos, sin, dq_next)
    return (handed_grad, key_grad, value_grad)


def solution(mesh):
    return jax.shard_map(
        shards,
        mesh=mesh,
        in_specs=(
            P("section", "ctx", None),
            P("section", "ctx", None),
            P("section", "ctx", None),
            P("section", "ctx", None),
            P("section", "ctx", None),
            P("ctx"),
            P("ctx", None),
        ),
        out_specs=(P("section", "ctx", None), P("section", "ctx", None), P("section", "ctx", None)),
        check_vma=False,
    )
```

time: 116 us -> 41.5 us (0.36)
  the two profiles are of different devices: /device:TPU:21 before, /device:TPU:14 now
where the time goes in v1:
time: 41.5 us; the launch traced here: 40.7 us
  waiting for transfers between devices  14.7 us (35%)
  starting transfers between devices  13.3 us (32%)
  Pallas kernels  11.9 us (29%)
  between operations  0.73 us (2%)
    ppermute x5, waiting for transfers between devices, from_behind(): lax.ppermute(value, axis, [(source, source + steps) for source in range(i...  14.7 us
    ppermute x5, starting transfers between devices, from_behind(): lax.ppermute(value, axis, [(source, source + steps) for source in range(i...  13.3 us
    pallas_call x1, Pallas kernels, shards(): pl.pallas_call(own_kernel, in_specs=[smem, vmem] + [hbm] * 5, out_specs=[...  4.5 us
    pallas_call x1, Pallas kernels, shards(): pl.pallas_call(cross_kernel, in_specs=[smem, smem] + [vmem] * 10, out_spe...  4.18 us
    pallas_call x1, Pallas kernels, shards(): pl.pallas_call(own_kv_kernel, in_specs=[vmem] * 4, out_specs=[vmem] * 2,...  1.21 us
    pallas_call x1, Pallas kernels, shards(): pl.pallas_call(sum_kernel, in_specs=[vmem] * 6 + [pl.BlockSpec(memory_spa...  1.08 us
    pallas_call x1, Pallas kernels, shards(): pl.pallas_call(pack_kernel, in_specs=[hbm, hbm], out_specs=vmem, out_shap...  0.96 us
  transfers between devices with their start and end apart: 5, of which 3 were waited for; matrix products, arithmetic and copies ran while one was open for 0% of the time, Pallas kernels for 14%

profile of v1, /device:TPU:14, one launch (start us, length us, event | category | flops | bytes accessed | tf_op | source)
XLA Modules:
  0.0 40.7 jit_solution(13781978611561358377)
XLA Ops:
  0.6 0.0 copy-start
  0.6 0.0 copy-start.1
  0.7 1.0 %pack_keys.1 = bf16[2,4,128,128]{3,2,1,0:T(8,128)(2,1)S(1)} custom-call(bf16[128,512]{1,0:T(8,128)(2,1)} %bitcast.12, bf16[128,512]{1,0:T(8,128)(2,1)} %bitcast.14), custom_call_target="tpu_custom_call" | custom-call | bytes 524288 | tf_op jit(solution)/shard_map/pack_keys/pallas_call | solution.py:341
  1.6 3.5 %collective-permute-start.1 = (bf16[2,4,128,128]{3,2,1,0:T(8,128)(2,1)S(1)}, bf16[2,4,128,128]{3,2,1,0:T(8,128)(2,1)S(1)}, u32[]{:S(2)}, u32[]{:S(2)}) collective-permute-start(bf16[2,4,128,128]{3,2,1,0:T(8,128)(2,1)S(1)} %pack_keys.1), channel_id=1, source_target_pairs={{0,4},{4,8},{8,12},{12,16},{16,20},{20,24},{24,28},{1,5},{5,9},{9,... | collective-permute-start | bytes 786440 | tf_op jit(solution)/shard_map/ppermute | solution.py:32
  5.1 3.5 %collective-permute-start = (bf16[2,4,128,128]{3,2,1,0:T(8,128)(2,1)S(1)}, bf16[2,4,128,128]{3,2,1,0:T(8,128)(2,1)S(1)}, u32[]{:S(2)}, u32[]{:S(2)}) collective-permute-start(bf16[2,4,128,128]{3,2,1,0:T(8,128)(2,1)S(1)} %pack_keys.1), channel_id=1, source_target_pairs={{0,8},{4,12},{8,16},{12,20},{16,24},{20,28},{1,9},{5,13},{9,17},{1... | collective-permute-start | bytes 786440 | tf_op jit(solution)/shard_map/ppermute | solution.py:32
  8.6 4.5 %own_block.1 = (bf16[16,256,256]{2,1,0:T(8,128)(2,1)S(1)}, bf16[4,128,1024]{2,1,0:T(8,128)(2,1)S(1)}, bf16[4,128,1024]{2,1,0:T(8,128)(2,1)S(1)}, bf16[4,128,128]...) custom-call(s32[1]{0:T(128)} %bitcast.first_ref, ...), custom_call_target="tpu_custom_call" | custom-call | flops 402653184 | bytes 9437184 | tf_op jit(solution)/shard_map/own_block/pallas_call | solution.py:354
  13.1 0.0 collective-permute-done.1.kv1_ref
  13.1 4.1 %collective-permute-done.kv2_ref = bf16[2,4,128,128]{3,2,1,0:T(8,128)(2,1)S(1)} collective-permute-done((bf16[2,4,128,128]{3,2,1,0:T(8,128)(2,1)S(1)}, bf16[2,4,128,128]{3,2,1,0:T(8,128)(2,1)S(1)}, u32[]{:S(2)}, u32[]{:S(2)}) %collective-permute-start) | collective-permute-done | bytes 262176 | tf_op jit(solution)/shard_map/ppermute | solution.py:32
  17.1 0.0 copy-done
  17.1 0.0 copy-done.1
  17.1 4.2 %cross_blocks.1 = (bf16[1,128,4096]{2,1,0:T(8,128)(2,1)S(1)}, bf16[2,4,128,128]{3,2,1,0:T(8,128)(2,1)S(1)}, bf16[2,4,128,128]{3,2,1,0:T(8,128)(2,1)S(1)}, f32[4,...) custom-call(s32[1]{0:T(128)} %bitcast.first_ref, s32[1,2]{1,0:T(1,128)S(1)} %copy-done.1, s32[1,128]{1,0:T(1,128)S(1)} %bitcast.8, ...), custom_call_target="tpu_custom_call" | custom-call | flops 1342177280 | bytes 6291456 | tf_op jit(solution)/shard_map/cross_blocks/pallas_call | solution.py:383
  21.3 1.9 %collective-permute-start.4 = (bf16[1,128,4096]{2,1,0:T(8,128)(2,1)S(1)}, bf16[1,128,4096]{2,1,0:T(8,128)(2,1)S(1)}, u32[]{:S(2)}, u32[]{:S(2)}) collective-permute-start(bf16[1,128,4096]{2,1,0:T(8,128)(2,1)S(1)} %get-tuple-element.39), channel_id=1, source_target_pairs={{1,0},{2,1},{3,2},{5,4},{6,5},{7,6},{9,8},{10,9},{11,10},{13,12},{... | collective-permute-start | bytes 3145736 | tf_op jit(solution)/shard_map/ppermute | solution.py:32
  23.3 1.9 %collective-permute-start.2 = (bf16[2,4,128,128]{3,2,1,0:T(8,128)(2,1)S(1)}, bf16[2,4,128,128]{3,2,1,0:T(8,128)(2,1)S(1)}, u32[]{:S(2)}, u32[]{:S(2)}) collective-permute-start(bf16[2,4,128,128]{3,2,1,0:T(8,128)(2,1)S(1)} %get-tuple-element.35), channel_id=1, source_target_pairs={{8,0},{12,4},{16,8},{20,12},{24,16},{28,20},{9,1},{13,5},{17,9},{2... | collective-permute-start | bytes 786440 | tf_op jit(solution)/shard_map/ppermute | solution.py:32
  25.2 2.5 %collective-permute-start.3 = (bf16[2,4,128,128]{3,2,1,0:T(8,128)(2,1)S(1)}, bf16[2,4,128,128]{3,2,1,0:T(8,128)(2,1)S(1)}, u32[]{:S(2)}, u32[]{:S(2)}) collective-permute-start(bf16[2,4,128,128]{3,2,1,0:T(8,128)(2,1)S(1)} %get-tuple-element.36), channel_id=1, source_target_pairs={{4,0},{8,4},{12,8},{16,12},{20,16},{24,20},{28,24},{5,1},{9,5},{13... | collective-permute-start | bytes 786440 | tf_op jit(solution)/shard_map/ppermute | solution.py:32
  27.7 1.2 %own_keys.1 = (f32[4,128,128]{2,1,0:T(8,128)S(1)}, f32[4,128,128]{2,1,0:T(8,128)S(1)}) custom-call(bf16[16,256,256]{2,1,0:T(8,128)(2,1)S(1)} %get-tuple-element.23.qg_ref, bf16[4,128,1024]{2,1,0:T(8,128)(2,1)S(1)} %get-tuple-element.24.prob_ref, bf16[4,128,1024]{2,1,0:T(8,128)(2,1)S(1)} %get-tuple-element.31.ds_ref, ...), custom_call_target="tpu_custom_call" | custom-call | flops 268435456 | bytes 5242880 | tf_op jit(solution)/shard_map/own_keys/pallas_call | solution.py:407
  28.9 5.0 %collective-permute-done.2.ret2_ref = bf16[2,4,128,128]{3,2,1,0:T(8,128)(2,1)S(1)} collective-permute-done((bf16[2,4,128,128]{3,2,1,0:T(8,128)(2,1)S(1)}, bf16[2,4,128,128]{3,2,1,0:T(8,128)(2,1)S(1)}, u32[]{:S(2)}, u32[]{:S(2)}) %collective-permute-start.2) | collective-permute-done | bytes 262176 | tf_op jit(solution)/shard_map/ppermute | solution.py:32
  33.9 5.7 %collective-permute-done.3.ret1_ref = bf16[2,4,128,128]{3,2,1,0:T(8,128)(2,1)S(1)} collective-permute-done((bf16[2,4,128,128]{3,2,1,0:T(8,128)(2,1)S(1)}, bf16[2,4,128,128]{3,2,1,0:T(8,128)(2,1)S(1)}, u32[]{:S(2)}, u32[]{:S(2)}) %collective-permute-start.3) | collective-permute-done | bytes 262176 | tf_op jit(solution)/shard_map/ppermute | solution.py:32
  39.6 0.0 collective-permute-done.4.dq_ref
  39.6 1.1 %sum_keys.1 = (bf16[1,128,512]{2,1,0:T(8,128)(2,1)}, bf16[1,128,512]{2,1,0:T(8,128)(2,1)}, bf16[1,128,4096]{2,1,0:T(8,128)(2,1)}) custom-call(f32[4,128,128]{2,1,0:T(8,128)S(1)} %get-tuple-element.33.dk_ref, f32[4,128,128]{2,1,0:T(8,128)S(1)} %get-tuple-element.34.dv_ref, bf16[2,4,128,128]{3,2,1,0:T(8,128)(2,1)S(1)} %collective-permute-done.2.ret2_ref, ...), custom_call_target="tpu_custom_call" | custom-call | bytes 3145728 | tf_op jit(solution)/shard_map/sum_keys/pallas_call | solution.py:417
Async XLA Ops:
  0.6 16.5 %copy-start = (s32[128]{0:T(128)S(1)}, s32[128]{0:T(128)}, u32[]{:S(2)}) copy-start(s32[128]{0:T(128)} %param.12) | copy-start | bytes 1540
  0.6 16.5 %copy-start.1 = (s32[1,2]{1,0:T(1,128)S(1)}, s32[1,2]{1,0:T(1,128)}, u32[]{:S(2)}) copy-start(s32[1,2]{1,0:T(1,128)} %list_ref.1) | copy-start | bytes 28
  1.6 11.5 %collective-permute-start.1 = (bf16[2,4,128,128]{3,2,1,0:T(8,128)(2,1)S(1)}, bf16[2,4,128,128]{3,2,1,0:T(8,128)(2,1)S(1)}, u32[]{:S(2)}, u32[]{:S(2)}) collective-permute-start(bf16[2,4,128,128]{3,2,1,0:T(8,128)(2,1)S(1)} %pack_keys.1), channel_id=1, source_target_pairs={{0,4},{4,8},{8,12},{12,16},{16,20},{20,24},{24,28},{1,5},{5,9},{9,... | collective-permute-start | bytes 786440 | tf_op jit(solution)/shard_map/ppermute | solution.py:32
  5.1 12.1 %collective-permute-start = (bf16[2,4,128,128]{3,2,1,0:T(8,128)(2,1)S(1)}, bf16[2,4,128,128]{3,2,1,0:T(8,128)(2,1)S(1)}, u32[]{:S(2)}, u32[]{:S(2)}) collective-permute-start(bf16[2,4,128,128]{3,2,1,0:T(8,128)(2,1)S(1)} %pack_keys.1), channel_id=1, source_target_pairs={{0,8},{4,12},{8,16},{12,20},{16,24},{20,28},{1,9},{5,13},{9,17},{1... | collective-permute-start | bytes 786440 | tf_op jit(solution)/shard_map/ppermute | solution.py:32
  21.3 18.2 %collective-permute-start.4 = (bf16[1,128,4096]{2,1,0:T(8,128)(2,1)S(1)}, bf16[1,128,4096]{2,1,0:T(8,128)(2,1)S(1)}, u32[]{:S(2)}, u32[]{:S(2)}) collective-permute-start(bf16[1,128,4096]{2,1,0:T(8,128)(2,1)S(1)} %get-tuple-element.39), channel_id=1, source_target_pairs={{1,0},{2,1},{3,2},{5,4},{6,5},{7,6},{9,8},{10,9},{11,10},{13,12},{... | collective-permute-start | bytes 3145736 | tf_op jit(solution)/shard_map/ppermute | solution.py:32
  23.3 10.7 %collective-permute-start.2 = (bf16[2,4,128,128]{3,2,1,0:T(8,128)(2,1)S(1)}, bf16[2,4,128,128]{3,2,1,0:T(8,128)(2,1)S(1)}, u32[]{:S(2)}, u32[]{:S(2)}) collective-permute-start(bf16[2,4,128,128]{3,2,1,0:T(8,128)(2,1)S(1)} %get-tuple-element.35), channel_id=1, source_target_pairs={{8,0},{12,4},{16,8},{20,12},{24,16},{28,20},{9,1},{13,5},{17,9},{2... | collective-permute-start | bytes 786440 | tf_op jit(solution)/shard_map/ppermute | solution.py:32
  25.2 14.4 %collective-permute-start.3 = (bf16[2,4,128,128]{3,2,1,0:T(8,128)(2,1)S(1)}, bf16[2,4,128,128]{3,2,1,0:T(8,128)(2,1)S(1)}, u32[]{:S(2)}, u32[]{:S(2)}) collective-permute-start(bf16[2,4,128,128]{3,2,1,0:T(8,128)(2,1)S(1)} %get-tuple-element.36), channel_id=1, source_target_pairs={{4,0},{8,4},{12,8},{16,12},{20,16},{24,20},{28,24},{5,1},{9,5},{13... | collective-permute-start | bytes 786440 | tf_op jit(solution)/shard_map/ppermute | solution.py:32

commit v2 on v1

--- a/solution.py
+++ b/solution.py
@@ -107,7 +107,7 @@
 
 def own_kernel(
     first_ref, doc_ref, q_hbm, k_hbm, v_hbm, o_hbm, g_hbm,
-    qg_ref, prob_ref, ds_ref, kt_ref, stat_ref, half_ref, cos_ref, sin_ref, cos12_ref, sin12_ref,
+    qg_ref, prob_ref, ds_ref, kt_ref, stat_ref, half_ref, cos_ref, sin_ref, cos1_ref, sin1_ref, cos2_ref, sin2_ref,
     q_ref, k_ref, v_ref, o_ref, g_ref, arrived,
 ):
     rows = q_hbm.shape[0]
@@ -130,11 +130,8 @@
     half_ref[1] = sin_t * SCORE_SCALE
     cos_ref[...], sin_ref[...] = upright(cos_t, sin_t)
     reach = doc_row[:, 0:1]
-    for distance in range(FETCH, 0, -1):
-        at = slice((FETCH - distance) * rows, (FETCH - distance + 1) * rows)
-        back_cos, back_sin = upright(*half_tables(columns - distance * rows - reach))
-        cos12_ref[at, :] = back_cos
-        sin12_ref[at, :] = back_sin
+    cos1_ref[...], sin1_ref[...] = upright(*half_tables(columns - rows - reach))
+    cos2_ref[...], sin2_ref[...] = upright(*half_tables(columns - 2 * rows - reach))
     key_idx = lax.broadcasted_iota(jnp.int32, (rows, rows), 0)
     query_idx = lax.broadcasted_iota(jnp.int32, (rows, rows), 1)
     mask = (key_idx <= query_idx) & (key_idx >= doc_row)
@@ -188,39 +185,131 @@
             finish(first, *now)
 
 
-def cross_kernel(
-    first_ref, list_ref, doc_ref, qg_ref, kv2_ref, kv1_ref, ds0_ref, kt_ref, stat_ref, half_ref, cos12_ref, sin12_ref,
-    dq_ref, ret2_ref, ret1_ref, scale_ref, own_ref, prob_buf, ds_buf,
+def reach_bias(listed, distance, doc_row, rows):
+    key_idx = lax.broadcasted_iota(jnp.int32, (rows, PAIR * rows), 0)
+    start = jnp.where(listed == 1, -distance * rows, -(1 << 30))
+    return jnp.where(key_idx + start >= doc_row[:, 0:1], 0.0, NEG_LARGE)
+
+
+def softmax_step(scores, stat_ref, group, at, in_reach):
+    before = stat_ref[group, 0:1, at]
+    largest = jnp.maximum(before, jnp.max(scores, axis=0, keepdims=True))
+    prob = jnp.exp2((scores - jnp.where(in_reach, largest, -NEG_LARGE)) * EXP2_SCALE)
+    largest = jnp.where(in_reach, largest, before)
+    scale = jnp.exp2((before - largest) * EXP2_SCALE)
+    total = stat_ref[group, 1:2, at] * scale + jnp.sum(prob, axis=0, keepdims=True)
+    return prob, largest, total, scale
+
+
+def staged(products, middle, finish):
+    ahead = products(0)
+    behind = None
+    for first in range(0, RATIO, PAIR):
+        now = ahead
+        if first + PAIR < RATIO:
+            ahead = products(first + PAIR)
+        done = middle(first, *now)
+        if behind is not None:
+            finish(first - PAIR, behind)
+        behind = done
+    finish(RATIO - PAIR, behind)
+
+
+def store_query_grad(dq_ref, group, first, dq, half_ref):
+    cos_t = jnp.concatenate([half_ref[0]] * PAIR, axis=1)
+    sin_t = jnp.concatenate([half_ref[1]] * PAIR, axis=1)
+    upper, lower = dq[:HALF], dq[HALF:]
+    dq = jnp.concatenate([upper * cos_t + lower * sin_t, lower * cos_t - upper * sin_t], axis=0).astype(BF16)
+    for i in range(PAIR):
+        lanes = pl.ds(pl.multiple_of((group * RATIO + first + i) * HD, HD), HD)
+        dq_ref[0, :, lanes] = dq[:, head_columns(i)].T
+
+
+def key_products(qg_ref, group, dscore, prob):
+    dk = dot_nn(dscore, group_rows(qg_ref, group, slice(HD))) * SCORE_SCALE
+    dv = dot_nn(prob, group_rows(qg_ref, group, slice(HD, 2 * HD)))
+    return dk.astype(BF16), dv.astype(BF16)
+
+
+def near_kernel(
+    first_ref, list_ref, doc_ref, qg_ref, kv_ref, ds0_ref, kt0_ref, stat_ref, half_ref, cos_ref, sin_ref,
+    dq_ref, ret2_ref, ret1_ref, scale_ref, own_ref, prob_ref, ds_ref, kt_ref, next_ref,
 ):
     rows = doc_ref.shape[1]
     doc_row = doc_ref[...] - first_ref[0]
-    reach = doc_row[:, 0:1]
-    in_reach = jnp.where(doc_row == reach, 1.0, 0.0)
-    in_reach = jnp.concatenate([in_reach] * PAIR, axis=1)
-    key_idx = lax.broadcasted_iota(jnp.int32, (rows, PAIR * rows), 0)
-    far = jnp.where(list_ref[0, 1] == 1, -2 * rows, -(1 << 30))
-    near = jnp.where(list_ref[0, 0] == 1, -rows, -(1 << 30))
-    bias = jnp.concatenate([key_idx + far, key_idx + near], axis=0)
-    bias = jnp.where(bias >= reach, 0.0, NEG_LARGE)
-
-    def attend(skipped):
-        used = FETCH * rows - skipped
-        behind_by_two = rows - skipped
-        own_bias = bias[skipped:]
-
-        def key_rows(which, group):
-            near_rows = kv1_ref[which, group]
-            if behind_by_two == 0:
-                return near_rows
-            return jnp.concatenate([kv2_ref[which, group, skipped:, :], near_rows], axis=0)
-
+    in_reach = jnp.concatenate([doc_row == doc_row[:, 0:1]] * PAIR, axis=1)
+    bias = reach_bias(list_ref[0, 0], 1, doc_row, rows)
+
+    def attend(last):
         @pl.loop(0, HK)
         def _(group):
-            k_rot = rotate(key_rows(0, group).astype(F32), cos12_ref[skipped:, :], sin12_ref[skipped:, :])
-            k_rot_t = jnp.concatenate([k_rot.T.astype(BF16), kt_ref[group]], axis=1)
-            left = block_diagonal(k_rot.astype(BF16), key_rows(1, group))
-            cos_t = jnp.concatenate([half_ref[0]] * PAIR, axis=1)
-            sin_t = jnp.concatenate([half_ref[1]] * PAIR, axis=1)
+            k_rot = rotate(kv_ref[0, group].astype(F32), cos_ref[...], sin_ref[...])
+            k_rot_t = k_rot.T.astype(BF16)
+            left = block_diagonal(k_rot.astype(BF16), kv_ref[1, group])
+            both_t = jnp.concatenate([k_rot_t, kt0_ref[group]], axis=1)
+
+            def products(first):
+                both = dot_nt(left, qg_ref[group * (RATIO // PAIR) + first // PAIR])
+                return both[:rows], both[rows:]
+
+            def middle(first, scores, dprob):
+                at = slice(first * HD, (first + PAIR) * HD)
+                prob, largest, total, scale = softmax_step(scores + bias, stat_ref, group, at, in_reach)
+                delta = stat_ref[group, 2:3, at]
+                if last:
+                    inverse = 1.0 / total
+                    scale = scale * inverse
+                    prob = prob * inverse
+                    scale_ref[group, 0:1, at] = scale
+                prob = prob.astype(BF16)
+                dscore = prob * (dprob - delta).astype(BF16)
+                prob_ref[group, :, at] = prob
+                ds_ref[group, :, at] = dscore
+                if last:
+                    own_dscore = ds0_ref[group, :, at] * scale.astype(BF16)
+                    own_ref[group, :, at] = own_dscore
+                    return jnp.concatenate([dscore, own_dscore], axis=0)
+                next_ref[group, 0:1, at] = largest
+                next_ref[group, 1:2, at] = total
+                next_ref[group, 2:3, at] = delta
+                next_ref[group, 3:4, at] = scale
+                return None
+
+            def finish(first, dscore):
+                if last:
+                    store_query_grad(dq_ref, group, first, dot_nn(both_t, dscore), half_ref)
+
+            staged(products, middle, finish)
+            if last:
+                ret1_ref[0, group], ret1_ref[1, group] = key_products(qg_ref, group, ds_ref[group], prob_ref[group])
+                ret2_ref[0, group] = jnp.zeros((rows, HD), BF16)
+                ret2_ref[1, group] = jnp.zeros((rows, HD), BF16)
+            else:
+                kt_ref[group] = k_rot_t
+
+    pl.when(list_ref[0, 1] != 1)(lambda: attend(True))
+    pl.when(list_ref[0, 1] == 1)(lambda: attend(False))
+
+
+def far_kernel(
+    first_ref, list_ref, doc_ref, qg_ref, kv_ref, ds0_ref, kt0_ref, half_ref, cos_ref, sin_ref,
+    prob1_ref, ds1_ref, kt1_ref, stat_ref, *refs,
+):
+    dq_ref, ret2_ref, ret1_ref, scale_ref, own_ref, prob_buf, ds_buf = refs[5:]
+    rows = doc_ref.shape[1]
+    doc_row = doc_ref[...] - first_ref[0]
+    in_reach = jnp.concatenate([doc_row == doc_row[:, 0:1]] * PAIR, axis=1)
+
+    def attend(skipped):
+        used = rows - skipped
+        bias = reach_bias(list_ref[0, 1], 2, doc_row, rows)[skipped:]
+
+        @pl.loop(0, HK)
+        def _(group):
+            k_rot = rotate(kv_ref[0, group, skipped:, :].astype(F32), cos_ref[skipped:, :], sin_ref[skipped:, :])
+            left = block_diagonal(k_rot.astype(BF16), kv_ref[1, group, skipped:, :])
+            k_rot_t = k_rot.T.astype(BF16)
+            near_t = jnp.concatenate([kt1_ref[group], kt0_ref[group]], axis=1)
 
             def products(first):
                 both = dot_nt(left, qg_ref[group * (RATIO // PAIR) + first // PAIR])
@@ -228,58 +317,40 @@
 
             def middle(first, scores, dprob):
                 at = slice(first * HD, (first + PAIR) * HD)
-                own_max = stat_ref[group, 0:1, at]
-                own_sum = stat_ref[group, 1:2, at]
-                delta = stat_ref[group, 2:3, at]
-                scores = scores + own_bias
-                largest = jnp.maximum(own_max, jnp.max(scores, axis=0, keepdims=True))
-                prob = jnp.exp2((scores - largest) * EXP2_SCALE)
-                total = jnp.sum(prob, axis=0, keepdims=True) * in_reach
-                own_scale = jnp.exp2(jnp.where(in_reach > 0.0, own_max - largest, 0.0) * EXP2_SCALE)
-                inverse = 1.0 / (own_sum * own_scale + total)
-                own_scale = own_scale * inverse
+                prob, _, total, scale = softmax_step(scores + bias, stat_ref, group, at, in_reach)
+                inverse = 1.0 / total
+                near_scale = scale * inverse
+                own_scale = near_scale * stat_ref[group, 3:4, at]
                 scale_ref[group, 0:1, at] = own_scale
-                prob = (prob * (inverse * in_reach)).astype(BF16)
-                dscore = prob * (dprob - delta).astype(BF16)
-                prob_buf[:used, at] = prob
-                ds_buf[:used, at] = dscore
+                prob = (prob * inverse).astype(BF16)
+                dscore = prob * (dprob - stat_ref[group, 2:3, at]).astype(BF16)
+                near_scale = near_scale.astype(BF16)
+                near_dscore = ds1_ref[group, :, at] * near_scale
                 own_dscore = ds0_ref[group, :, at] * own_scale.astype(BF16)
                 own_ref[group, :, at] = own_dscore
-                return jnp.concatenate([dscore, own_dscore], axis=0)
-
-            def finish(first, dscore):
-                dq = dot_nn(k_rot_t, dscore)
-                upper, lower = dq[:HALF], dq[HALF:]
-                dq = jnp.concatenate([upper * cos_t + lower * sin_t, lower * cos_t - upper * sin_t], axis=0)
-                dq = dq.astype(BF16)
-                for i in range(PAIR):
-                    lanes = pl.ds(pl.multiple_of((group * RATIO + first + i) * HD, HD), HD)
-                    dq_ref[0, :, lanes] = dq[:, head_columns(i)].T
-
-            ahead = products(0)
-            behind = None
-            for first in range(0, RATIO, PAIR):
-                now = ahead
-                if first + PAIR < RATIO:
-                    ahead = products(first + PAIR)
-                done = middle(first, *now)
-                if behind is not None:
-                    finish(first - PAIR, behind)
-                behind = done
-            finish(RATIO - PAIR, behind)
-            dk = dot_nn(ds_buf[:used, :], group_rows(qg_ref, group, slice(HD))) * SCORE_SCALE
-            dv = dot_nn(prob_buf[:used, :], group_rows(qg_ref, group, slice(HD, 2 * HD)))
-            for which, grad in enumerate((dk.astype(BF16), dv.astype(BF16))):
-                ret1_ref[which, group] = grad[behind_by_two:]
+                prob_buf[:used, at] = prob
+                prob_buf[used : used + rows, at] = prob1_ref[group, :, at] * near_scale
+                ds_buf[:used, at] = dscore
+                ds_buf[used : used + rows, at] = near_dscore
+                return dscore, jnp.concatenate([near_dscore, own_dscore], axis=0)
+
+            def finish(first, dscores):
+                dq = dot_nn(near_t, dscores[1]) + dot_nn(k_rot_t, dscores[0])
+                store_query_grad(dq_ref, group, first, dq, half_ref)
+
+            staged(products, middle, finish)
+            grads = key_products(qg_ref, group, ds_buf[: used + rows, :], prob_buf[: used + rows, :])
+            for which, grad in enumerate(grads):
+                ret1_ref[which, group] = grad[used:]
+                ret2_ref[which, group, skipped:, :] = grad[:used]
                 if skipped:
                     ret2_ref[which, group, :skipped, :] = jnp.zeros((skipped, HD), BF16)
-                if behind_by_two:
-                    ret2_ref[which, group, skipped:, :] = grad[:behind_by_two]
-
-    farthest = jnp.min(doc_row.astype(F32))
-    pl.when(farthest >= -rows)(lambda: attend(rows))
-    pl.when((farthest < -rows) & (farthest >= -rows - rows // 2))(lambda: attend(rows // 2))
-    pl.when(farthest < -rows - rows // 2)(lambda: attend(0))
+
+    @pl.when(list_ref[0, 1] == 1)
+    def _():
+        farthest = jnp.min(doc_row.astype(F32))
+        pl.when(farthest >= -rows - rows // 2)(lambda: attend(rows // 2))
+        pl.when(farthest < -rows - rows // 2)(lambda: attend(0))
 
 
 def own_kv_kernel(qg_ref, prob_ref, ds_ref, scale_ref, dk_ref, dv_ref):
@@ -351,10 +422,10 @@
     kv2 = from_behind(kv, "ctx", 2)
     kv1 = from_behind(kv, "ctx", 1)
 
-    qg, prob0, ds0, k_own_t, stat, half, cos, sin, cos12, sin12 = pl.pallas_call(
+    qg, prob0, ds0, k_own_t, stat, half, cos, sin, cos1, sin1, cos2, sin2 = pl.pallas_call(
         own_kernel,
         in_specs=[smem, vmem] + [hbm] * 5,
-        out_specs=[vmem] * 10,
+        out_specs=[vmem] * 12,
         out_shape=[
             shape((HQ // PAIR, PAIR * rows, 2 * HD), BF16),
             shape((HK, rows, RATIO * rows), BF16),
@@ -364,8 +435,10 @@
             shape((2, HALF, rows), F32),
             shape((rows, HD), F32),
             shape((rows, HD), F32),
-            shape((FETCH * rows, HD), F32),
-            shape((FETCH * rows, HD), F32),
+            shape((rows, HD), F32),
+            shape((rows, HD), F32),
+            shape((rows, HD), F32),
+            shape((rows, HD), F32),
         ],
         scratch_shapes=[
             pltpu.VMEM((HK, rows, wide), BF16),
@@ -380,26 +453,46 @@
         name="own_block",
     )(first_row, pltpu.with_memory_space_constraint(doc_row, pltpu.HBM), *arguments)
 
+    results = [
+        shape((1, rows, HQ * HD), BF16),
+        shape((2, HK, rows, HD), BF16),
+        shape((2, HK, rows, HD), BF16),
+        shape((HK, 8, RATIO * rows), F32),
+        shape((HK, rows, RATIO * rows), BF16),
+    ]
+    *settled, prob1, ds1, k_near_t, stat1 = pl.pallas_call(
+        near_kernel,
+        in_specs=[smem, smem] + [vmem] * 9,
+        out_specs=[vmem] * 9,
+        out_shape=results
+        + [
+            shape((HK, rows, RATIO * rows), BF16),
+            shape((HK, rows, RATIO * rows), BF16),
+            shape((HK, HD, rows), BF16),
+            shape((HK, 8, RATIO * rows), F32),
+        ],
+        compiler_params=params,
+        cost_estimate=cost(5 * block_flops, 9 * 2**20, HQ * rows * rows),
+        name="near_block",
+    )(first_row, fetch_list, doc_row, qg, kv1, ds0, k_own_t, stat, half, cos1, sin1)
+
     dq, ret2, ret1, scale, ds_own = pl.pallas_call(
-        cross_kernel,
-        in_specs=[smem, smem] + [vmem] * 10,
+        far_kernel,
+        in_specs=[smem, smem] + [vmem] * 17,
         out_specs=[vmem] * 5,
-        out_shape=[
-            shape((1, rows, HQ * HD), BF16),
-            shape((2, HK, rows, HD), BF16),
-            shape((2, HK, rows, HD), BF16),
-            shape((HK, 8, RATIO * rows), F32),
-            shape((HK, rows, RATIO * rows), BF16),
-        ],
+        out_shape=results,
         scratch_shapes=[
             pltpu.VMEM((FETCH * rows, RATIO * rows), BF16),
             pltpu.VMEM((FETCH * rows, RATIO * rows), BF16),
         ],
+        input_output_aliases={14 + i: i for i in range(5)},
         compiler_params=params,
-        cost_estimate=cost(10 * block_flops, 6 * 2**20, 2 * HQ * rows * rows),
-        name="cross_blocks",
-    )(first_row, fetch_list, doc_row, qg, kv2, kv1, ds0, k_own_t, stat, half, cos12, sin12)
-
+        cost_estimate=cost(5 * block_flops, 9 * 2**20, HQ * rows * rows),
+        name="far_block",
+    )(
+        first_row, fetch_list, doc_row, qg, kv2, ds0, k_own_t, half, cos2, sin2,
+        prob1, ds1, k_near_t, stat1, *settled,
+    )
     arrived1 = from_behind(ret1, "ctx", -1)
     arrived2 = from_behind(ret2, "ctx", -2)
     dq_next = from_behind(dq, "section", -1)

time: 41.5 us -> 40.7 us (0.981); the launches traced: 40.7 us -> 40.4 us
  waiting for transfers between devices: 14.7 us -> 10.7 us
  starting transfers between devices: 13.3 us -> 16.1 us
  Pallas kernels: 11.9 us -> 12.8 us
    ppermute x5, waiting for transfers between devices: 14.7 us -> 10.7 us  [from_behind(): lax.ppermute(value, axis, [(source, source + steps) for source in range(i...]
    ppermute x5, starting transfers between devices: 13.3 us -> 16.1 us  [from_behind(): lax.ppermute(value, axis, [(source, source + steps) for source in range(i...]
    pallas_call x1 -> x2, Pallas kernels: 4.18 us -> 4.81 us  [the longest x1 4.18 us: shards(): pl.pallas_call(near_kernel, in_specs=[smem, smem] + [vmem] * 9, out_specs...]
  transfers between devices with their start and end apart: 5 -> 5, of which waited for: 3 -> 2; matrix products, arithmetic and copies ran while one was open for 0% -> 0% of each run, Pallas kernels for 14% -> 25%
where the time goes in v2:
time: 40.7 us; the launch traced here: 40.4 us
  starting transfers between devices  16.1 us (40%)
  Pallas kernels  12.8 us (31%)
  waiting for transfers between devices  10.7 us (26%)
  between operations  0.76 us (2%)
    ppermute x5, starting transfers between devices, from_behind(): lax.ppermute(value, axis, [(source, source + steps) for source in range(i...  16.1 us
    ppermute x5, waiting for transfers between devices, from_behind(): lax.ppermute(value, axis, [(source, source + steps) for source in range(i...  10.7 us
    pallas_call x1, Pallas kernels, shards(): pl.pallas_call(own_kernel, in_specs=[smem, vmem] + [hbm] * 5, out_specs=[...  4.77 us
    pallas_call x1, Pallas kernels, shards(): pl.pallas_call(near_kernel, in_specs=[smem, smem] + [vmem] * 9, out_specs...  4.18 us
    pallas_call x1, Pallas kernels, shards(): pl.pallas_call(own_kv_kernel, in_specs=[vmem] * 4, out_specs=[vmem] * 2,...  1.18 us
    pallas_call x1, Pallas kernels, shards(): pl.pallas_call(sum_kernel, in_specs=[vmem] * 6 + [pl.BlockSpec(memory_spa...  1.08 us
    pallas_call x1, Pallas kernels, shards(): pl.pallas_call(pack_kernel, in_specs=[hbm, hbm], out_specs=vmem, out_shap...  0.96 us
  transfers between devices with their start and end apart: 5, of which 2 were waited for; matrix products, arithmetic and copies ran while one was open for 0% of the time, Pallas kernels for 25%

profile of v2, /device:TPU:14, one launch (start us, length us, event | category | flops | bytes accessed | tf_op | source)
XLA Modules:
  0.0 40.4 jit_solution(18221961307026716084)
XLA Ops:
  0.6 0.0 copy-start
  0.6 0.0 copy-start.1
  0.7 1.0 %pack_keys.1 = bf16[2,4,128,128]{3,2,1,0:T(8,128)(2,1)S(1)} custom-call(bf16[128,512]{1,0:T(8,128)(2,1)} %bitcast.13, bf16[128,512]{1,0:T(8,128)(2,1)} %bitcast.15), custom_call_target="tpu_custom_call" | custom-call | bytes 524288 | tf_op jit(solution)/shard_map/pack_keys/pallas_call | solution.py:412
  1.6 3.5 %collective-permute-start.1 = (bf16[2,4,128,128]{3,2,1,0:T(8,128)(2,1)S(1)}, bf16[2,4,128,128]{3,2,1,0:T(8,128)(2,1)S(1)}, u32[]{:S(2)}, u32[]{:S(2)}) collective-permute-start(bf16[2,4,128,128]{3,2,1,0:T(8,128)(2,1)S(1)} %pack_keys.1), channel_id=1, source_target_pairs={{0,4},{4,8},{8,12},{12,16},{16,20},{20,24},{24,28},{1,5},{5,9},{9,... | collective-permute-start | bytes 786440 | tf_op jit(solution)/shard_map/ppermute | solution.py:32
  5.1 3.5 %collective-permute-start = (bf16[2,4,128,128]{3,2,1,0:T(8,128)(2,1)S(1)}, bf16[2,4,128,128]{3,2,1,0:T(8,128)(2,1)S(1)}, u32[]{:S(2)}, u32[]{:S(2)}) collective-permute-start(bf16[2,4,128,128]{3,2,1,0:T(8,128)(2,1)S(1)} %pack_keys.1), channel_id=1, source_target_pairs={{0,8},{4,12},{8,16},{12,20},{16,24},{20,28},{1,9},{5,13},{9,17},{1... | collective-permute-start | bytes 786440 | tf_op jit(solution)/shard_map/ppermute | solution.py:32
  8.6 4.8 %own_block.1 = (bf16[16,256,256]{2,1,0:T(8,128)(2,1)S(1)}, bf16[4,128,1024]{2,1,0:T(8,128)(2,1)S(1)}, bf16[4,128,1024]{2,1,0:T(8,128)(2,1)S(1)}, bf16[4,128,128]...) custom-call(s32[1]{0:T(128)} %bitcast.first_ref, ...), custom_call_target="tpu_custom_call" | custom-call | flops 402653184 | bytes 9437184 | tf_op jit(solution)/shard_map/own_block/pallas_call | solution.py:425
  13.4 0.0 collective-permute-done.1.kv_ref
  13.4 0.0 copy-done
  13.4 0.0 copy-done.1
  13.4 4.2 %near_block.1 = (bf16[1,128,4096]{2,1,0:T(8,128)(2,1)S(1)}, bf16[2,4,128,128]{3,2,1,0:T(8,128)(2,1)S(1)}, bf16[2,4,128,128]{3,2,1,0:T(8,128)(2,1)S(1)}, f32[4,8,...) custom-call(s32[1]{0:T(128)} %bitcast.first_ref, ...), custom_call_target="tpu_custom_call" | custom-call | flops 671088640 | bytes 9437184 | tf_op jit(solution)/shard_map/near_block/pallas_call | solution.py:463
  17.6 0.0 collective-permute-done.kv_ref
  17.6 0.6 %far_block.1 = (bf16[1,128,4096]{2,1,0:T(8,128)(2,1)S(1)}, bf16[2,4,128,128]{3,2,1,0:T(8,128)(2,1)S(1)}, bf16[2,4,128,128]{3,2,1,0:T(8,128)(2,1)S(1)}, f32[4,8,1...) custom-call(s32[1]{0:T(128)} %bitcast.first_ref, ...), custom_call_target="tpu_custom_call", output_to_operand_aliasing={{0}: (14, {}), {1}: (15, {}), {2}: (16, {}), {3}: (17, {}),... | custom-call | flops 671088640 | bytes 9437184 | tf_op jit(solution)/shard_map/far_block/pallas_call | solution.py:479
  18.2 1.9 %collective-permute-start.4 = (bf16[1,128,4096]{2,1,0:T(8,128)(2,1)S(1)}, bf16[1,128,4096]{2,1,0:T(8,128)(2,1)S(1)}, u32[]{:S(2)}, u32[]{:S(2)}) collective-permute-start(bf16[1,128,4096]{2,1,0:T(8,128)(2,1)S(1)} %get-tuple-element.61), channel_id=1, source_target_pairs={{1,0},{2,1},{3,2},{5,4},{6,5},{7,6},{9,8},{10,9},{11,10},{13,12},{... | collective-permute-start | bytes 3145736 | tf_op jit(solution)/shard_map/ppermute | solution.py:32
  20.1 2.4 %collective-permute-start.2 = (bf16[2,4,128,128]{3,2,1,0:T(8,128)(2,1)S(1)}, bf16[2,4,128,128]{3,2,1,0:T(8,128)(2,1)S(1)}, u32[]{:S(2)}, u32[]{:S(2)}) collective-permute-start(bf16[2,4,128,128]{3,2,1,0:T(8,128)(2,1)S(1)} %get-tuple-element.57), channel_id=1, source_target_pairs={{8,0},{12,4},{16,8},{20,12},{24,16},{28,20},{9,1},{13,5},{17,9},{2... | collective-permute-start | bytes 786440 | tf_op jit(solution)/shard_map/ppermute | solution.py:32
  22.5 4.9 %collective-permute-start.3 = (bf16[2,4,128,128]{3,2,1,0:T(8,128)(2,1)S(1)}, bf16[2,4,128,128]{3,2,1,0:T(8,128)(2,1)S(1)}, u32[]{:S(2)}, u32[]{:S(2)}) collective-permute-start(bf16[2,4,128,128]{3,2,1,0:T(8,128)(2,1)S(1)} %get-tuple-element.58), channel_id=1, source_target_pairs={{4,0},{8,4},{12,8},{16,12},{20,16},{24,20},{28,24},{5,1},{9,5},{13... | collective-permute-start | bytes 786440 | tf_op jit(solution)/shard_map/ppermute | solution.py:32
  27.4 1.2 %own_keys.1 = (f32[4,128,128]{2,1,0:T(8,128)S(1)}, f32[4,128,128]{2,1,0:T(8,128)S(1)}) custom-call(bf16[16,256,256]{2,1,0:T(8,128)(2,1)S(1)} %get-tuple-element.34.qg_ref, bf16[4,128,1024]{2,1,0:T(8,128)(2,1)S(1)} %get-tuple-element.35.prob_ref, bf16[4,128,1024]{2,1,0:T(8,128)(2,1)S(1)} %get-tuple-element.53.ds_ref, ...), custom_call_target="tpu_custom_call" | custom-call | flops 268435456 | bytes 5242880 | tf_op jit(solution)/shard_map/own_keys/pallas_call | solution.py:500
  28.6 2.2 %collective-permute-done.2.ret2_ref = bf16[2,4,128,128]{3,2,1,0:T(8,128)(2,1)S(1)} collective-permute-done((bf16[2,4,128,128]{3,2,1,0:T(8,128)(2,1)S(1)}, bf16[2,4,128,128]{3,2,1,0:T(8,128)(2,1)S(1)}, u32[]{:S(2)}, u32[]{:S(2)}) %collective-permute-start.2) | collective-permute-done | bytes 262176 | tf_op jit(solution)/shard_map/ppermute | solution.py:32
  30.8 8.5 %collective-permute-done.3.ret1_ref = bf16[2,4,128,128]{3,2,1,0:T(8,128)(2,1)S(1)} collective-permute-done((bf16[2,4,128,128]{3,2,1,0:T(8,128)(2,1)S(1)}, bf16[2,4,128,128]{3,2,1,0:T(8,128)(2,1)S(1)}, u32[]{:S(2)}, u32[]{:S(2)}) %collective-permute-start.3) | collective-permute-done | bytes 262176 | tf_op jit(solution)/shard_map/ppermute | solution.py:32
  39.3 0.0 collective-permute-done.4.dq_ref
  39.3 1.1 %sum_keys.1 = (bf16[1,128,512]{2,1,0:T(8,128)(2,1)}, bf16[1,128,512]{2,1,0:T(8,128)(2,1)}, bf16[1,128,4096]{2,1,0:T(8,128)(2,1)}) custom-call(f32[4,128,128]{2,1,0:T(8,128)S(1)} %get-tuple-element.55.dk_ref, f32[4,128,128]{2,1,0:T(8,128)S(1)} %get-tuple-element.56.dv_ref, bf16[2,4,128,128]{3,2,1,0:T(8,128)(2,1)S(1)} %collective-permute-done.2.ret2_ref, ...), custom_call_target="tpu_custom_call" | custom-call | bytes 3145728 | tf_op jit(solution)/shard_map/sum_keys/pallas_call | solution.py:510
Async XLA Ops:
  0.6 12.7 %copy-start = (s32[128]{0:T(128)S(1)}, s32[128]{0:T(128)}, u32[]{:S(2)}) copy-start(s32[128]{0:T(128)} %param.12) | copy-start | bytes 1540
  0.6 12.7 %copy-start.1 = (s32[1,2]{1,0:T(1,128)S(1)}, s32[1,2]{1,0:T(1,128)}, u32[]{:S(2)}) copy-start(s32[1,2]{1,0:T(1,128)} %list_ref.3) | copy-start | bytes 28
  1.6 11.7 %collective-permute-start.1 = (bf16[2,4,128,128]{3,2,1,0:T(8,128)(2,1)S(1)}, bf16[2,4,128,128]{3,2,1,0:T(8,128)(2,1)S(1)}, u32[]{:S(2)}, u32[]{:S(2)}) collective-permute-start(bf16[2,4,128,128]{3,2,1,0:T(8,128)(2,1)S(1)} %pack_keys.1), channel_id=1, source_target_pairs={{0,4},{4,8},{8,12},{12,16},{16,20},{20,24},{24,28},{1,5},{5,9},{9,... | collective-permute-start | bytes 786440 | tf_op jit(solution)/shard_map/ppermute | solution.py:32
  5.1 12.5 %collective-permute-start = (bf16[2,4,128,128]{3,2,1,0:T(8,128)(2,1)S(1)}, bf16[2,4,128,128]{3,2,1,0:T(8,128)(2,1)S(1)}, u32[]{:S(2)}, u32[]{:S(2)}) collective-permute-start(bf16[2,4,128,128]{3,2,1,0:T(8,128)(2,1)S(1)} %pack_keys.1), channel_id=1, source_target_pairs={{0,8},{4,12},{8,16},{12,20},{16,24},{20,28},{1,9},{5,13},{9,17},{1... | collective-permute-start | bytes 786440 | tf_op jit(solution)/shard_map/ppermute | solution.py:32
  18.2 21.1 %collective-permute-start.4 = (bf16[1,128,4096]{2,1,0:T(8,128)(2,1)S(1)}, bf16[1,128,4096]{2,1,0:T(8,128)(2,1)S(1)}, u32[]{:S(2)}, u32[]{:S(2)}) collective-permute-start(bf16[1,128,4096]{2,1,0:T(8,128)(2,1)S(1)} %get-tuple-element.61), channel_id=1, source_target_pairs={{1,0},{2,1},{3,2},{5,4},{6,5},{7,6},{9,8},{10,9},{11,10},{13,12},{... | collective-permute-start | bytes 3145736 | tf_op jit(solution)/shard_map/ppermute | solution.py:32
  20.1 10.7 %collective-permute-start.2 = (bf16[2,4,128,128]{3,2,1,0:T(8,128)(2,1)S(1)}, bf16[2,4,128,128]{3,2,1,0:T(8,128)(2,1)S(1)}, u32[]{:S(2)}, u32[]{:S(2)}) collective-permute-start(bf16[2,4,128,128]{3,2,1,0:T(8,128)(2,1)S(1)} %get-tuple-element.57), channel_id=1, source_target_pairs={{8,0},{12,4},{16,8},{20,12},{24,16},{28,20},{9,1},{13,5},{17,9},{2... | collective-permute-start | bytes 786440 | tf_op jit(solution)/shard_map/ppermute | solution.py:32
  22.5 16.8 %collective-permute-start.3 = (bf16[2,4,128,128]{3,2,1,0:T(8,128)(2,1)S(1)}, bf16[2,4,128,128]{3,2,1,0:T(8,128)(2,1)S(1)}, u32[]{:S(2)}, u32[]{:S(2)}) collective-permute-start(bf16[2,4,128,128]{3,2,1,0:T(8,128)(2,1)S(1)} %get-tuple-element.58), channel_id=1, source_target_pairs={{4,0},{8,4},{12,8},{16,12},{20,16},{24,20},{28,24},{5,1},{9,5},{13... | collective-permute-start | bytes 786440 | tf_op jit(solution)/shard_map/ppermute | solution.py:32

commit v3 on v2

--- a/solution.py
+++ b/solution.py
@@ -106,8 +106,8 @@
 
 
 def own_kernel(
-    first_ref, doc_ref, q_hbm, k_hbm, v_hbm, o_hbm, g_hbm,
-    qg_ref, prob_ref, ds_ref, kt_ref, stat_ref, half_ref, cos_ref, sin_ref, cos1_ref, sin1_ref, cos2_ref, sin2_ref,
+    first_ref, list_ref, doc_ref, q_hbm, k_hbm, v_hbm, o_hbm, g_hbm,
+    notes_ref, qg_ref, prob_ref, ds_ref, kt_ref, stat_ref, half_ref, cos_ref, sin_ref, cos1_ref, sin1_ref, cos2_ref, sin2_ref,
     q_ref, k_ref, v_ref, o_ref, g_ref, arrived,
 ):
     rows = q_hbm.shape[0]
@@ -130,6 +130,10 @@
     half_ref[1] = sin_t * SCORE_SCALE
     cos_ref[...], sin_ref[...] = upright(cos_t, sin_t)
     reach = doc_row[:, 0:1]
+    notes_ref[0:1, :] = doc_row.astype(F32)
+    for distance in range(1, FETCH + 1):
+        listed = jnp.where(list_ref[:, distance - 1 : distance] == 1, 1.0, 0.0)
+        notes_ref[distance : distance + 1, :] = jnp.broadcast_to(listed, (1, rows))
     cos1_ref[...], sin1_ref[...] = upright(*half_tables(columns - rows - reach))
     cos2_ref[...], sin2_ref[...] = upright(*half_tables(columns - 2 * rows - reach))
     key_idx = lax.broadcasted_iota(jnp.int32, (rows, rows), 0)
@@ -185,10 +189,17 @@
             finish(first, *now)
 
 
-def reach_bias(listed, distance, doc_row, rows):
-    key_idx = lax.broadcasted_iota(jnp.int32, (rows, PAIR * rows), 0)
-    start = jnp.where(listed == 1, -distance * rows, -(1 << 30))
-    return jnp.where(key_idx + start >= doc_row[:, 0:1], 0.0, NEG_LARGE)
+def reach_bias(notes_ref, distance):
+    rows = notes_ref.shape[1]
+    key_idx = lax.broadcasted_iota(jnp.int32, (rows, PAIR * rows), 0).astype(F32) - distance * rows
+    reach = notes_ref[0:1, 0:1]
+    listed = notes_ref[distance : distance + 1, 0:1]
+    return jnp.where((key_idx >= reach) & (listed > 0.0), 0.0, NEG_LARGE)
+
+
+def reached(notes_ref):
+    doc_row = notes_ref[0:1, :]
+    return jnp.concatenate([doc_row == doc_row[:, 0:1]] * PAIR, axis=1)
 
 
 def softmax_step(scores, stat_ref, group, at, in_reach):
@@ -232,16 +243,15 @@
 
 
 def near_kernel(
-    first_ref, list_ref, doc_ref, qg_ref, kv_ref, ds0_ref, kt0_ref, stat_ref, half_ref, cos_ref, sin_ref,
+    notes_ref, qg_ref, kv_ref, ds0_ref, kt0_ref, stat_ref, half_ref, cos_ref, sin_ref,
     dq_ref, ret2_ref, ret1_ref, scale_ref, own_ref, prob_ref, ds_ref, kt_ref, next_ref,
 ):
-    rows = doc_ref.shape[1]
-    doc_row = doc_ref[...] - first_ref[0]
-    in_reach = jnp.concatenate([doc_row == doc_row[:, 0:1]] * PAIR, axis=1)
-    bias = reach_bias(list_ref[0, 0], 1, doc_row, rows)
+    rows = notes_ref.shape[1]
+    in_reach = reached(notes_ref)
+    bias = reach_bias(notes_ref, 1)
 
     def attend(last):
-        @pl.loop(0, HK)
+        @pl.loop(0, HK, unroll=2)
         def _(group):
             k_rot = rotate(kv_ref[0, group].astype(F32), cos_ref[...], sin_ref[...])
             k_rot_t = k_rot.T.astype(BF16)
@@ -287,24 +297,24 @@
             else:
                 kt_ref[group] = k_rot_t
 
-    pl.when(list_ref[0, 1] != 1)(lambda: attend(True))
-    pl.when(list_ref[0, 1] == 1)(lambda: attend(False))
+    goes_on = jnp.max(notes_ref[2:3, :]) > 0.0
+    pl.when(jnp.logical_not(goes_on))(lambda: attend(True))
+    pl.when(goes_on)(lambda: attend(False))
 
 
 def far_kernel(
-    first_ref, list_ref, doc_ref, qg_ref, kv_ref, ds0_ref, kt0_ref, half_ref, cos_ref, sin_ref,
+    notes_ref, qg_ref, kv_ref, ds0_ref, kt0_ref, half_ref, cos_ref, sin_ref,
     prob1_ref, ds1_ref, kt1_ref, stat_ref, *refs,
 ):
     dq_ref, ret2_ref, ret1_ref, scale_ref, own_ref, prob_buf, ds_buf = refs[5:]
-    rows = doc_ref.shape[1]
-    doc_row = doc_ref[...] - first_ref[0]
-    in_reach = jnp.concatenate([doc_row == doc_row[:, 0:1]] * PAIR, axis=1)
+    rows = notes_ref.shape[1]
 
     def attend(skipped):
         used = rows - skipped
-        bias = reach_bias(list_ref[0, 1], 2, doc_row, rows)[skipped:]
-
-        @pl.loop(0, HK)
+        in_reach = reached(notes_ref)
+        bias = reach_bias(notes_ref, 2)[skipped:]
+
+        @pl.loop(0, HK, unroll=2)
         def _(group):
             k_rot = rotate(kv_ref[0, group, skipped:, :].astype(F32), cos_ref[skipped:, :], sin_ref[skipped:, :])
             left = block_diagonal(k_rot.astype(BF16), kv_ref[1, group, skipped:, :])
@@ -346,9 +356,9 @@
                 if skipped:
                     ret2_ref[which, group, :skipped, :] = jnp.zeros((skipped, HD), BF16)
 
-    @pl.when(list_ref[0, 1] == 1)
+    @pl.when(jnp.max(notes_ref[2:3, :]) > 0.0)
     def _():
-        farthest = jnp.min(doc_row.astype(F32))
+        farthest = jnp.min(notes_ref[0:1, :])
         pl.when(farthest >= -rows - rows // 2)(lambda: attend(rows // 2))
         pl.when(farthest < -rows - rows // 2)(lambda: attend(0))
 
@@ -422,11 +432,12 @@
     kv2 = from_behind(kv, "ctx", 2)
     kv1 = from_behind(kv, "ctx", 1)
 
-    qg, prob0, ds0, k_own_t, stat, half, cos, sin, cos1, sin1, cos2, sin2 = pl.pallas_call(
+    notes, qg, prob0, ds0, k_own_t, stat, half, cos, sin, cos1, sin1, cos2, sin2 = pl.pallas_call(
         own_kernel,
-        in_specs=[smem, vmem] + [hbm] * 5,
-        out_specs=[vmem] * 12,
+        in_specs=[smem, vmem, vmem] + [hbm] * 5,
+        out_specs=[vmem] * 13,
         out_shape=[
+            shape((8, rows), F32),
             shape((HQ // PAIR, PAIR * rows, 2 * HD), BF16),
             shape((HK, rows, RATIO * rows), BF16),
             shape((HK, rows, RATIO * rows), BF16),
@@ -451,7 +462,7 @@
         compiler_params=params,
         cost_estimate=cost(3 * block_flops, 9 * 2**20, HQ * rows * rows),
         name="own_block",
-    )(first_row, pltpu.with_memory_space_constraint(doc_row, pltpu.HBM), *arguments)
+    )(first_row, *(pltpu.with_memory_space_constraint(x, pltpu.HBM) for x in (fetch_list, doc_row)), *arguments)
 
     results = [
         shape((1, rows, HQ * HD), BF16),
@@ -462,7 +473,7 @@
     ]
     *settled, prob1, ds1, k_near_t, stat1 = pl.pallas_call(
         near_kernel,
-        in_specs=[smem, smem] + [vmem] * 9,
+        in_specs=[vmem] * 9,
         out_specs=[vmem] * 9,
         out_shape=results
         + [
@@ -474,25 +485,22 @@
         compiler_params=params,
         cost_estimate=cost(5 * block_flops, 9 * 2**20, HQ * rows * rows),
         name="near_block",
-    )(first_row, fetch_list, doc_row, qg, kv1, ds0, k_own_t, stat, half, cos1, sin1)
+    )(notes, qg, kv1, ds0, k_own_t, stat, half, cos1, sin1)
 
     dq, ret2, ret1, scale, ds_own = pl.pallas_call(
         far_kernel,
-        in_specs=[smem, smem] + [vmem] * 17,
+        in_specs=[vmem] * 17,
         out_specs=[vmem] * 5,
         out_shape=results,
         scratch_shapes=[
             pltpu.VMEM((FETCH * rows, RATIO * rows), BF16),
             pltpu.VMEM((FETCH * rows, RATIO * rows), BF16),
         ],
-        input_output_aliases={14 + i: i for i in range(5)},
+        input_output_aliases={12 + i: i for i in range(5)},
         compiler_params=params,
         cost_estimate=cost(5 * block_flops, 9 * 2**20, HQ * rows * rows),
         name="far_block",
-    )(
-        first_row, fetch_list, doc_row, qg, kv2, ds0, k_own_t, half, cos2, sin2,
-        prob1, ds1, k_near_t, stat1, *settled,
-    )
+    )(notes, qg, kv2, ds0, k_own_t, half, cos2, sin2, prob1, ds1, k_near_t, stat1, *settled)
     arrived1 = from_behind(ret1, "ctx", -1)
     arrived2 = from_behind(ret2, "ctx", -2)
     dq_next = from_behind(dq, "section", -1)

time: 40.7 us -> 39 us (0.958)
  Pallas kernels: 12.8 us -> 11.3 us
  starting transfers between devices: 16.1 us -> 15.3 us
  waiting for transfers between devices: 10.7 us -> 11.3 us
    pallas_call x3, Pallas kernels: 9.58 us -> 8.08 us  [the longest x1 4.75 us: shards(): pl.pallas_call(own_kernel, in_specs=[smem, vmem, vmem] + [hbm] * 5, out_s...]
    ppermute x5, starting transfers between devices: 16.1 us -> 15.3 us  [from_behind(): lax.ppermute(value, axis, [(source, source + steps) for source in range(i...]
    ppermute x5, waiting for transfers between devices: 10.7 us -> 11.3 us  [from_behind(): lax.ppermute(value, axis, [(source, source + steps) for source in range(i...]
  transfers between devices with their start and end apart: 5 -> 5, of which waited for: 2 -> 3; matrix products, arithmetic and copies ran while one was open for 0% -> 0% of each run, Pallas kernels for 25% -> 24%
where the time goes in v3:
time: 39 us; the launch traced here: 38.6 us
  starting transfers between devices  15.3 us (39%)
  Pallas kernels  11.3 us (29%)
  waiting for transfers between devices  11.3 us (29%)
  between operations  0.72 us (2%)
    ppermute x5, starting transfers between devices, from_behind(): lax.ppermute(value, axis, [(source, source + steps) for source in range(i...  15.3 us
    ppermute x5, waiting for transfers between devices, from_behind(): lax.ppermute(value, axis, [(source, source + steps) for source in range(i...  11.3 us
    pallas_call x1, Pallas kernels, shards(): pl.pallas_call(own_kernel, in_specs=[smem, vmem, vmem] + [hbm] * 5, out_s...  4.75 us
    pallas_call x1, Pallas kernels, shards(): pl.pallas_call(near_kernel, in_specs=[vmem] * 9, out_specs=[vmem] * 9, ou...  3.21 us
    pallas_call x1, Pallas kernels, shards(): pl.pallas_call(own_kv_kernel, in_specs=[vmem] * 4, out_specs=[vmem] * 2,...  1.18 us
    pallas_call x1, Pallas kernels, shards(): pl.pallas_call(sum_kernel, in_specs=[vmem] * 6 + [pl.BlockSpec(memory_spa...  1.08 us
    pallas_call x1, Pallas kernels, shards(): pl.pallas_call(pack_kernel, in_specs=[hbm, hbm], out_specs=vmem, out_shap...  0.95 us
  transfers between devices with their start and end apart: 5, of which 3 were waited for; matrix products, arithmetic and copies ran while one was open for 0% of the time, Pallas kernels for 24%

profile of v3, /device:TPU:14, one launch (start us, length us, event | category | flops | bytes accessed | tf_op | source)
XLA Modules:
  0.0 38.6 jit_solution(5358189896060770997)
XLA Ops:
  0.6 0.9 %pack_keys.1 = bf16[2,4,128,128]{3,2,1,0:T(8,128)(2,1)S(1)} custom-call(bf16[128,512]{1,0:T(8,128)(2,1)} %bitcast.10, bf16[128,512]{1,0:T(8,128)(2,1)} %bitcast.12), custom_call_target="tpu_custom_call" | custom-call | bytes 524288 | tf_op jit(solution)/shard_map/pack_keys/pallas_call | solution.py:422
  1.6 3.5 %collective-permute-start.1 = (bf16[2,4,128,128]{3,2,1,0:T(8,128)(2,1)S(1)}, bf16[2,4,128,128]{3,2,1,0:T(8,128)(2,1)S(1)}, u32[]{:S(2)}, u32[]{:S(2)}) collective-permute-start(bf16[2,4,128,128]{3,2,1,0:T(8,128)(2,1)S(1)} %pack_keys.1), channel_id=1, source_target_pairs={{0,4},{4,8},{8,12},{12,16},{16,20},{20,24},{24,28},{1,5},{5,9},{9,... | collective-permute-start | bytes 786440 | tf_op jit(solution)/shard_map/ppermute | solution.py:32
  5.0 3.5 %collective-permute-start = (bf16[2,4,128,128]{3,2,1,0:T(8,128)(2,1)S(1)}, bf16[2,4,128,128]{3,2,1,0:T(8,128)(2,1)S(1)}, u32[]{:S(2)}, u32[]{:S(2)}) collective-permute-start(bf16[2,4,128,128]{3,2,1,0:T(8,128)(2,1)S(1)} %pack_keys.1), channel_id=1, source_target_pairs={{0,8},{4,12},{8,16},{12,20},{16,24},{20,28},{1,9},{5,13},{9,17},{1... | collective-permute-start | bytes 786440 | tf_op jit(solution)/shard_map/ppermute | solution.py:32
  8.5 4.7 %own_block.1 = (f32[8,128]{1,0:T(8,128)S(1)}, bf16[16,256,256]{2,1,0:T(8,128)(2,1)S(1)}, bf16[4,128,1024]{2,1,0:T(8,128)(2,1)S(1)}, bf16[4,128,1024]{2,1,0:T(8,1...) custom-call(s32[1]{0:T(128)} %bitcast.first_ref, ...), custom_call_target="tpu_custom_call" | custom-call | flops 402653184 | bytes 9437184 | tf_op jit(solution)/shard_map/own_block/pallas_call | solution.py:435
  13.3 0.0 collective-permute-done.1.kv_ref
  13.3 3.2 %near_block.1 = (bf16[1,128,4096]{2,1,0:T(8,128)(2,1)S(1)}, bf16[2,4,128,128]{3,2,1,0:T(8,128)(2,1)S(1)}, bf16[2,4,128,128]{3,2,1,0:T(8,128)(2,1)S(1)}, f32[4,8,...) custom-call(f32[8,128]{1,0:T(8,128)S(1)} %get-tuple-element.37.notes, ...), custom_call_target="tpu_custom_call" | custom-call | flops 671088640 | bytes 9437184 | tf_op jit(solution)/shard_map/near_block/pallas_call | solution.py:474
  16.5 0.6 %collective-permute-done.kv_ref = bf16[2,4,128,128]{3,2,1,0:T(8,128)(2,1)S(1)} collective-permute-done((bf16[2,4,128,128]{3,2,1,0:T(8,128)(2,1)S(1)}, bf16[2,4,128,128]{3,2,1,0:T(8,128)(2,1)S(1)}, u32[]{:S(2)}, u32[]{:S(2)}) %collective-permute-start) | collective-permute-done | bytes 262176 | tf_op jit(solution)/shard_map/ppermute | solution.py:32
  17.1 0.1 far_block.1
  17.2 1.9 %collective-permute-start.4 = (bf16[1,128,4096]{2,1,0:T(8,128)(2,1)S(1)}, bf16[1,128,4096]{2,1,0:T(8,128)(2,1)S(1)}, u32[]{:S(2)}, u32[]{:S(2)}) collective-permute-start(bf16[1,128,4096]{2,1,0:T(8,128)(2,1)S(1)} %get-tuple-element.63), channel_id=1, source_target_pairs={{1,0},{2,1},{3,2},{5,4},{6,5},{7,6},{9,8},{10,9},{11,10},{13,12},{... | collective-permute-start | bytes 3145736 | tf_op jit(solution)/shard_map/ppermute | solution.py:32
  19.2 1.9 %collective-permute-start.2 = (bf16[2,4,128,128]{3,2,1,0:T(8,128)(2,1)S(1)}, bf16[2,4,128,128]{3,2,1,0:T(8,128)(2,1)S(1)}, u32[]{:S(2)}, u32[]{:S(2)}) collective-permute-start(bf16[2,4,128,128]{3,2,1,0:T(8,128)(2,1)S(1)} %get-tuple-element.59), channel_id=1, source_target_pairs={{8,0},{12,4},{16,8},{20,12},{24,16},{28,20},{9,1},{13,5},{17,9},{2... | collective-permute-start | bytes 786440 | tf_op jit(solution)/shard_map/ppermute | solution.py:32
  21.1 4.5 %collective-permute-start.3 = (bf16[2,4,128,128]{3,2,1,0:T(8,128)(2,1)S(1)}, bf16[2,4,128,128]{3,2,1,0:T(8,128)(2,1)S(1)}, u32[]{:S(2)}, u32[]{:S(2)}) collective-permute-start(bf16[2,4,128,128]{3,2,1,0:T(8,128)(2,1)S(1)} %get-tuple-element.60), channel_id=1, source_target_pairs={{4,0},{8,4},{12,8},{16,12},{20,16},{24,20},{28,24},{5,1},{9,5},{13... | collective-permute-start | bytes 786440 | tf_op jit(solution)/shard_map/ppermute | solution.py:32
  25.7 1.2 %own_keys.1 = (f32[4,128,128]{2,1,0:T(8,128)S(1)}, f32[4,128,128]{2,1,0:T(8,128)S(1)}) custom-call(bf16[16,256,256]{2,1,0:T(8,128)(2,1)S(1)} %get-tuple-element.35.qg_ref, bf16[4,128,1024]{2,1,0:T(8,128)(2,1)S(1)} %get-tuple-element.36.prob_ref, bf16[4,128,1024]{2,1,0:T(8,128)(2,1)S(1)} %get-tuple-element.55.ds_ref, ...), custom_call_target="tpu_custom_call" | custom-call | flops 268435456 | bytes 5242880 | tf_op jit(solution)/shard_map/own_keys/pallas_call | solution.py:508
  26.8 6.4 %collective-permute-done.2.ret2_ref = bf16[2,4,128,128]{3,2,1,0:T(8,128)(2,1)S(1)} collective-permute-done((bf16[2,4,128,128]{3,2,1,0:T(8,128)(2,1)S(1)}, bf16[2,4,128,128]{3,2,1,0:T(8,128)(2,1)S(1)}, u32[]{:S(2)}, u32[]{:S(2)}) %collective-permute-start.2) | collective-permute-done | bytes 262176 | tf_op jit(solution)/shard_map/ppermute | solution.py:32
  33.2 4.3 %collective-permute-done.3.ret1_ref = bf16[2,4,128,128]{3,2,1,0:T(8,128)(2,1)S(1)} collective-permute-done((bf16[2,4,128,128]{3,2,1,0:T(8,128)(2,1)S(1)}, bf16[2,4,128,128]{3,2,1,0:T(8,128)(2,1)S(1)}, u32[]{:S(2)}, u32[]{:S(2)}) %collective-permute-start.3) | collective-permute-done | bytes 262176 | tf_op jit(solution)/shard_map/ppermute | solution.py:32
  37.5 0.0 collective-permute-done.4.dq_ref
  37.5 1.1 %sum_keys.1 = (bf16[1,128,512]{2,1,0:T(8,128)(2,1)}, bf16[1,128,512]{2,1,0:T(8,128)(2,1)}, bf16[1,128,4096]{2,1,0:T(8,128)(2,1)}) custom-call(f32[4,128,128]{2,1,0:T(8,128)S(1)} %get-tuple-element.57.dk_ref, f32[4,128,128]{2,1,0:T(8,128)S(1)} %get-tuple-element.58.dv_ref, bf16[2,4,128,128]{3,2,1,0:T(8,128)(2,1)S(1)} %collective-permute-done.2.ret2_ref, ...), custom_call_target="tpu_custom_call" | custom-call | bytes 3145728 | tf_op jit(solution)/shard_map/sum_keys/pallas_call | solution.py:518
Async XLA Ops:
  1.6 11.7 %collective-permute-start.1 = (bf16[2,4,128,128]{3,2,1,0:T(8,128)(2,1)S(1)}, bf16[2,4,128,128]{3,2,1,0:T(8,128)(2,1)S(1)}, u32[]{:S(2)}, u32[]{:S(2)}) collective-permute-start(bf16[2,4,128,128]{3,2,1,0:T(8,128)(2,1)S(1)} %pack_keys.1), channel_id=1, source_target_pairs={{0,4},{4,8},{8,12},{12,16},{16,20},{20,24},{24,28},{1,5},{5,9},{9,... | collective-permute-start | bytes 786440 | tf_op jit(solution)/shard_map/ppermute | solution.py:32
  5.0 12.1 %collective-permute-start = (bf16[2,4,128,128]{3,2,1,0:T(8,128)(2,1)S(1)}, bf16[2,4,128,128]{3,2,1,0:T(8,128)(2,1)S(1)}, u32[]{:S(2)}, u32[]{:S(2)}) collective-permute-start(bf16[2,4,128,128]{3,2,1,0:T(8,128)(2,1)S(1)} %pack_keys.1), channel_id=1, source_target_pairs={{0,8},{4,12},{8,16},{12,20},{16,24},{20,28},{1,9},{5,13},{9,17},{1... | collective-permute-start | bytes 786440 | tf_op jit(solution)/shard_map/ppermute | solution.py:32
  17.2 20.3 %collective-permute-start.4 = (bf16[1,128,4096]{2,1,0:T(8,128)(2,1)S(1)}, bf16[1,128,4096]{2,1,0:T(8,128)(2,1)S(1)}, u32[]{:S(2)}, u32[]{:S(2)}) collective-permute-start(bf16[1,128,4096]{2,1,0:T(8,128)(2,1)S(1)} %get-tuple-element.63), channel_id=1, source_target_pairs={{1,0},{2,1},{3,2},{5,4},{6,5},{7,6},{9,8},{10,9},{11,10},{13,12},{... | collective-permute-start | bytes 3145736 | tf_op jit(solution)/shard_map/ppermute | solution.py:32
  19.2 14.1 %collective-permute-start.2 = (bf16[2,4,128,128]{3,2,1,0:T(8,128)(2,1)S(1)}, bf16[2,4,128,128]{3,2,1,0:T(8,128)(2,1)S(1)}, u32[]{:S(2)}, u32[]{:S(2)}) collective-permute-start(bf16[2,4,128,128]{3,2,1,0:T(8,128)(2,1)S(1)} %get-tuple-element.59), channel_id=1, source_target_pairs={{8,0},{12,4},{16,8},{20,12},{24,16},{28,20},{9,1},{13,5},{17,9},{2... | collective-permute-start | bytes 786440 | tf_op jit(solution)/shard_map/ppermute | solution.py:32
  21.1 16.4 %collective-permute-start.3 = (bf16[2,4,128,128]{3,2,1,0:T(8,128)(2,1)S(1)}, bf16[2,4,128,128]{3,2,1,0:T(8,128)(2,1)S(1)}, u32[]{:S(2)}, u32[]{:S(2)}) collective-permute-start(bf16[2,4,128,128]{3,2,1,0:T(8,128)(2,1)S(1)} %get-tuple-element.60), channel_id=1, source_target_pairs={{4,0},{8,4},{12,8},{16,12},{20,16},{24,20},{28,24},{5,1},{9,5},{13... | collective-permute-start | bytes 786440 | tf_op jit(solution)/shard_map/ppermute | solution.py:32

commit v4 on v3

--- a/solution.py
+++ b/solution.py
@@ -13,7 +13,8 @@
 RATIO = HQ // HK
 HALF = HD // 2
 FETCH = 2
-PAIR = 2
+QUAD = 4
+TILES = 4
 
 ROPE_BASE = 1000000.0
 TRAINED_CONTEXT = 32768.0
@@ -77,8 +78,15 @@
     return slice(head * HD, (head + 1) * HD)
 
 
-def stack_heads(ref, group, first):
-    return jnp.concatenate([ref[group, :, head_columns(first + i)] for i in range(PAIR)], axis=0)
+def stack_heads(ref, group, first, half):
+    rows = ref.shape[1] // 2
+    at = slice(half * rows, (half + 1) * rows)
+    return jnp.concatenate([ref[group, at, head_columns(first + i)] for i in range(QUAD)], axis=0)
+
+
+def four_times(value, half):
+    columns = value.shape[1] // 2
+    return jnp.concatenate([value[:, half * columns : (half + 1) * columns]] * QUAD, axis=1)
 
 
 def block_diagonal(upper, lower):
@@ -88,9 +96,13 @@
     )
 
 
-def group_rows(ref, group, columns):
-    pairs = range(RATIO // PAIR)
-    return jnp.concatenate([ref[group * len(pairs) + i, :, columns] for i in pairs], axis=0)
+def group_rows(ref, group, columns, tiles=TILES):
+    return jnp.concatenate([ref[group * TILES + i, :, columns] for i in range(tiles)], axis=0)
+
+
+def tile_columns(tile):
+    width = RATIO * HD // TILES
+    return slice(tile * width, (tile + 1) * width)
 
 
 def pack_kernel(k_hbm, v_hbm, kv_ref, arrived):
@@ -126,80 +138,84 @@
     doc_row = doc_ref[...] - first_ref[0]
     columns = lax.broadcasted_iota(jnp.int32, (1, rows), 1)
     cos_t, sin_t = half_tables(columns - doc_row)
-    half_ref[0] = cos_t * SCORE_SCALE
-    half_ref[1] = sin_t * SCORE_SCALE
     cos_ref[...], sin_ref[...] = upright(cos_t, sin_t)
     reach = doc_row[:, 0:1]
-    notes_ref[0:1, :] = doc_row.astype(F32)
+    lanes = notes_ref.shape[1]
+    for half in range(2):
+        notes_ref[half : half + 1, :] = four_times(doc_row.astype(F32), half)
+        half_ref[half, 0] = four_times(cos_t * SCORE_SCALE, half)
+        half_ref[half, 1] = four_times(sin_t * SCORE_SCALE, half)
     for distance in range(1, FETCH + 1):
         listed = jnp.where(list_ref[:, distance - 1 : distance] == 1, 1.0, 0.0)
-        notes_ref[distance : distance + 1, :] = jnp.broadcast_to(listed, (1, rows))
+        notes_ref[distance + 1 : distance + 2, :] = jnp.broadcast_to(listed, (1, lanes))
     cos1_ref[...], sin1_ref[...] = upright(*half_tables(columns - rows - reach))
     cos2_ref[...], sin2_ref[...] = upright(*half_tables(columns - 2 * rows - reach))
     key_idx = lax.broadcasted_iota(jnp.int32, (rows, rows), 0)
     query_idx = lax.broadcasted_iota(jnp.int32, (rows, rows), 1)
     mask = (key_idx <= query_idx) & (key_idx >= doc_row)
     bias = jnp.where(mask, 0.0, NEG_LARGE)
-    bias = jnp.concatenate([bias] * PAIR, axis=1)
+    bias = [four_times(bias, half) for half in range(2)]
     ones = jnp.ones((8, HD), BF16)
 
     @pl.loop(0, HK)
     def _(group):
         for which in range(len(arguments)):
             fetch(which, group).wait()
-        cosine = cos_ref[...]
-        signed_sine = sin_ref[...]
-        k_rot = rotate(k_ref[group].astype(F32), cosine, signed_sine)
+        k_rot = rotate(k_ref[group].astype(F32), cos_ref[...], sin_ref[...])
         kt_ref[group] = k_rot.T.astype(BF16)
         left = block_diagonal(k_rot.astype(BF16), v_ref[group])
 
-        def products(first):
-            pair = group * (RATIO // PAIR) + first // PAIR
-            for i in range(PAIR):
-                rows_of = slice(i * rows, (i + 1) * rows)
-                q_rot = rotate(q_ref[group, :, head_columns(first + i)].astype(F32), cosine, signed_sine)
-                qg_ref[pair, rows_of, :HD] = q_rot.astype(BF16)
-            grads = stack_heads(g_ref, group, first)
-            qg_ref[pair, :, HD:] = grads
-            product = grads.astype(F32) * stack_heads(o_ref, group, first).astype(F32)
+        def products(tile):
+            half, quad = divmod(tile, 2)
+            at = slice(half * rows // 2, (half + 1) * rows // 2)
+            cosine = jnp.concatenate([cos_ref[at, :]] * QUAD, axis=0)
+            signed_sine = jnp.concatenate([sin_ref[at, :]] * QUAD, axis=0)
+            queries = stack_heads(q_ref, group, quad * QUAD, half).astype(F32)
+            qg_ref[group * TILES + tile, :, :HD] = rotate(queries, cosine, signed_sine).astype(BF16)
+            grads = stack_heads(g_ref, group, quad * QUAD, half)
+            qg_ref[group * TILES + tile, :, HD:] = grads
+            product = grads.astype(F32) * stack_heads(o_ref, group, quad * QUAD, half).astype(F32)
             high = product.astype(BF16)
             low = (product - high.astype(F32)).astype(BF16)
             delta = (dot_nt(ones, high) + dot_nt(ones, low))[0:1]
-            both = dot_nt(left, qg_ref[pair])
+            both = dot_nt(left, qg_ref[group * TILES + tile])
             return both[:rows], both[rows:], delta
 
-        def finish(first, scores, dprob, delta):
-            at = slice(first * HD, (first + PAIR) * HD)
-            scores = scores + bias
+        def finish(tile, scores, dprob, delta):
+            at = tile_columns(tile)
+            scores = scores + bias[tile // 2]
             largest = jnp.max(scores, axis=0, keepdims=True)
             prob = jnp.exp2((scores - largest) * EXP2_SCALE)
-            total = jnp.sum(prob, axis=0, keepdims=True)
-            dscore = (prob * (dprob - delta)).astype(BF16)
             prob_ref[group, :, at] = prob.astype(BF16)
-            ds_ref[group, :, at] = dscore
+            ds_ref[group, :, at] = (prob * (dprob - delta)).astype(BF16)
             stat_ref[group, 0:1, at] = largest
-            stat_ref[group, 1:2, at] = total
+            stat_ref[group, 1:2, at] = jnp.sum(prob, axis=0, keepdims=True)
             stat_ref[group, 2:3, at] = delta
 
         ahead = products(0)
-        for first in range(0, RATIO, PAIR):
+        for tile in range(TILES):
             now = ahead
-            if first + PAIR < RATIO:
-                ahead = products(first + PAIR)
-            finish(first, *now)
-
-
-def reach_bias(notes_ref, distance):
-    rows = notes_ref.shape[1]
-    key_idx = lax.broadcasted_iota(jnp.int32, (rows, PAIR * rows), 0).astype(F32) - distance * rows
-    reach = notes_ref[0:1, 0:1]
-    listed = notes_ref[distance : distance + 1, 0:1]
-    return jnp.where((key_idx >= reach) & (listed > 0.0), 0.0, NEG_LARGE)
+            if tile + 1 < TILES:
+                ahead = products(tile + 1)
+            finish(tile, *now)
+
+
+def reach_bias(notes_ref, distance, rows):
+    key_idx = lax.broadcasted_iota(jnp.int32, (rows, notes_ref.shape[1]), 0).astype(F32) - distance * rows
+    listed = notes_ref[distance + 1 : distance + 2, 0:1]
+    return jnp.where((key_idx >= notes_ref[0:1, 0:1]) & (listed > 0.0), 0.0, NEG_LARGE)
 
 
 def reached(notes_ref):
-    doc_row = notes_ref[0:1, :]
-    return jnp.concatenate([doc_row == doc_row[:, 0:1]] * PAIR, axis=1)
+    return [notes_ref[half : half + 1, :] == notes_ref[0:1, 0:1] for half in range(2)]
+
+
+def high_reached(notes_ref):
+    return jnp.max(jnp.where(notes_ref[1:2, :] == notes_ref[0:1, 0:1], 1.0, 0.0)) > 0.0
+
+
+def goes_on(notes_ref):
+    return jnp.max(notes_ref[3:4, :]) > 0.0
 
 
 def softmax_step(scores, stat_ref, group, at, in_reach):
@@ -212,33 +228,45 @@
     return prob, largest, total, scale
 
 
-def staged(products, middle, finish):
+def staged(tiles, products, middle, finish):
     ahead = products(0)
     behind = None
-    for first in range(0, RATIO, PAIR):
+    for tile in range(tiles):
         now = ahead
-        if first + PAIR < RATIO:
-            ahead = products(first + PAIR)
-        done = middle(first, *now)
+        if tile + 1 < tiles:
+            ahead = products(tile + 1)
+        done = middle(tile, *now)
         if behind is not None:
-            finish(first - PAIR, behind)
+            finish(tile - 1, behind)
         behind = done
-    finish(RATIO - PAIR, behind)
-
-
-def store_query_grad(dq_ref, group, first, dq, half_ref):
-    cos_t = jnp.concatenate([half_ref[0]] * PAIR, axis=1)
-    sin_t = jnp.concatenate([half_ref[1]] * PAIR, axis=1)
+    finish(tiles - 1, behind)
+
+
+def store_query_grad(dq_ref, group, tile, dq, half_ref):
+    half, quad = divmod(tile, 2)
+    rows = dq_ref.shape[1] // 2
+    cos_t, sin_t = half_ref[half, 0], half_ref[half, 1]
     upper, lower = dq[:HALF], dq[HALF:]
     dq = jnp.concatenate([upper * cos_t + lower * sin_t, lower * cos_t - upper * sin_t], axis=0).astype(BF16)
-    for i in range(PAIR):
-        lanes = pl.ds(pl.multiple_of((group * RATIO + first + i) * HD, HD), HD)
-        dq_ref[0, :, lanes] = dq[:, head_columns(i)].T
-
-
-def key_products(qg_ref, group, dscore, prob):
-    dk = dot_nn(dscore, group_rows(qg_ref, group, slice(HD))) * SCORE_SCALE
-    dv = dot_nn(prob, group_rows(qg_ref, group, slice(HD, 2 * HD)))
+    dq = dq.T
+    for i in range(QUAD):
+        head = group * RATIO + quad * QUAD + i
+        dq_ref[0, half * rows : (half + 1) * rows, head_columns(head)] = dq[i * rows : (i + 1) * rows]
+
+
+def own_alone(dq_ref, scale_ref, own_ref, ds0_ref, kt0_ref, stat_ref, half_ref, group, tiles):
+    for tile in tiles:
+        at = tile_columns(tile)
+        scale = 1.0 / stat_ref[group, 1:2, at]
+        scale_ref[group, 0:1, at] = scale
+        dscore = ds0_ref[group, :, at] * scale.astype(BF16)
+        own_ref[group, :, at] = dscore
+        store_query_grad(dq_ref, group, tile, dot_nn(kt0_ref[group], dscore), half_ref)
+
+
+def key_products(qg_ref, group, tiles, dscore, prob):
+    dk = dot_nn(dscore, group_rows(qg_ref, group, slice(HD), tiles)) * SCORE_SCALE
+    dv = dot_nn(prob, group_rows(qg_ref, group, slice(HD, 2 * HD), tiles))
     return dk.astype(BF16), dv.astype(BF16)
 
 
@@ -246,60 +274,71 @@
     notes_ref, qg_ref, kv_ref, ds0_ref, kt0_ref, stat_ref, half_ref, cos_ref, sin_ref,
     dq_ref, ret2_ref, ret1_ref, scale_ref, own_ref, prob_ref, ds_ref, kt_ref, next_ref,
 ):
-    rows = notes_ref.shape[1]
-    in_reach = reached(notes_ref)
-    bias = reach_bias(notes_ref, 1)
-
-    def attend(last):
-        @pl.loop(0, HK, unroll=2)
-        def _(group):
-            k_rot = rotate(kv_ref[0, group].astype(F32), cos_ref[...], sin_ref[...])
-            k_rot_t = k_rot.T.astype(BF16)
-            left = block_diagonal(k_rot.astype(BF16), kv_ref[1, group])
-            both_t = jnp.concatenate([k_rot_t, kt0_ref[group]], axis=1)
-
-            def products(first):
-                both = dot_nt(left, qg_ref[group * (RATIO // PAIR) + first // PAIR])
-                return both[:rows], both[rows:]
-
-            def middle(first, scores, dprob):
-                at = slice(first * HD, (first + PAIR) * HD)
-                prob, largest, total, scale = softmax_step(scores + bias, stat_ref, group, at, in_reach)
-                delta = stat_ref[group, 2:3, at]
-                if last:
-                    inverse = 1.0 / total
-                    scale = scale * inverse
-                    prob = prob * inverse
-                    scale_ref[group, 0:1, at] = scale
-                prob = prob.astype(BF16)
-                dscore = prob * (dprob - delta).astype(BF16)
-                prob_ref[group, :, at] = prob
-                ds_ref[group, :, at] = dscore
-                if last:
-                    own_dscore = ds0_ref[group, :, at] * scale.astype(BF16)
-                    own_ref[group, :, at] = own_dscore
-                    return jnp.concatenate([dscore, own_dscore], axis=0)
-                next_ref[group, 0:1, at] = largest
-                next_ref[group, 1:2, at] = total
-                next_ref[group, 2:3, at] = delta
-                next_ref[group, 3:4, at] = scale
-                return None
-
-            def finish(first, dscore):
-                if last:
-                    store_query_grad(dq_ref, group, first, dot_nn(both_t, dscore), half_ref)
-
-            staged(products, middle, finish)
+    rows = kv_ref.shape[2]
+
+    def attend(last, tiles):
+        in_reach = reached(notes_ref)
+        bias = reach_bias(notes_ref, 1, rows)
+        for group in range(HK):
+            one_group(last, tiles, in_reach, bias, group)
+
+    def one_group(last, tiles, in_reach, bias, group):
+        k_rot = rotate(kv_ref[0, group].astype(F32), cos_ref[...], sin_ref[...])
+        k_rot_t = k_rot.T.astype(BF16)
+        left = block_diagonal(k_rot.astype(BF16), kv_ref[1, group])
+        both_t = jnp.concatenate([k_rot_t, kt0_ref[group]], axis=1)
+
+        def products(tile):
+            both = dot_nt(left, qg_ref[group * TILES + tile])
+            return both[:rows], both[rows:]
+
+        def middle(tile, scores, dprob):
+            at = tile_columns(tile)
+            prob, largest, total, scale = softmax_step(scores + bias, stat_ref, group, at, in_reach[tile // 2])
+            delta = stat_ref[group, 2:3, at]
             if last:
-                ret1_ref[0, group], ret1_ref[1, group] = key_products(qg_ref, group, ds_ref[group], prob_ref[group])
-                ret2_ref[0, group] = jnp.zeros((rows, HD), BF16)
-                ret2_ref[1, group] = jnp.zeros((rows, HD), BF16)
-            else:
-                kt_ref[group] = k_rot_t
-
-    goes_on = jnp.max(notes_ref[2:3, :]) > 0.0
-    pl.when(jnp.logical_not(goes_on))(lambda: attend(True))
-    pl.when(goes_on)(lambda: attend(False))
+                inverse = 1.0 / total
+                scale = scale * inverse
+                prob = prob * inverse
+                scale_ref[group, 0:1, at] = scale
+            prob = prob.astype(BF16)
+            dscore = prob * (dprob - delta).astype(BF16)
+            prob_ref[group, :, at] = prob
+            ds_ref[group, :, at] = dscore
+            if last:
+                own_dscore = ds0_ref[group, :, at] * scale.astype(BF16)
+                own_ref[group, :, at] = own_dscore
+                return jnp.concatenate([dscore, own_dscore], axis=0)
+            next_ref[group, 0:1, at] = largest
+            next_ref[group, 1:2, at] = total
+            next_ref[group, 2:3, at] = delta
+            next_ref[group, 3:4, at] = scale
+            return None
+
+        def finish(tile, dscore):
+            if last:
+                store_query_grad(dq_ref, group, tile, dot_nn(both_t, dscore), half_ref)
+
+        staged(tiles, products, middle, finish)
+        if last:
+            own_alone(
+                dq_ref, scale_ref, own_ref, ds0_ref, kt0_ref, stat_ref, half_ref, group, range(tiles, TILES)
+            )
+            used = slice(0, tile_columns(tiles - 1).stop)
+            grads = key_products(qg_ref, group, tiles, ds_ref[group, :, used], prob_ref[group, :, used])
+            for which, grad in enumerate(grads):
+                ret1_ref[which, group] = grad
+                ret2_ref[which, group] = jnp.zeros((rows, HD), BF16)
+        else:
+            kt_ref[group] = k_rot_t
+            for tile in range(tiles, TILES):
+                next_ref[group, 1:2, tile_columns(tile)] = stat_ref[group, 1:2, tile_columns(tile)]
+
+    further, wide = goes_on(notes_ref), high_reached(notes_ref)
+    for last in (True, False):
+        for tiles in (TILES // 2, TILES):
+            chosen = (further != last) & (wide == (tiles == TILES))
+            pl.when(chosen)(lambda last=last, tiles=tiles: attend(last, tiles))
 
 
 def far_kernel(
@@ -307,60 +346,65 @@
     prob1_ref, ds1_ref, kt1_ref, stat_ref, *refs,
 ):
     dq_ref, ret2_ref, ret1_ref, scale_ref, own_ref, prob_buf, ds_buf = refs[5:]
-    rows = notes_ref.shape[1]
-
-    def attend(skipped):
+    rows = kv_ref.shape[2]
+
+    def attend(skipped, tiles):
+        in_reach = reached(notes_ref)
+        bias = reach_bias(notes_ref, 2, rows)[skipped:]
+        for group in range(HK):
+            one_group(skipped, tiles, in_reach, bias, group)
+
+    def one_group(skipped, tiles, in_reach, bias, group):
         used = rows - skipped
-        in_reach = reached(notes_ref)
-        bias = reach_bias(notes_ref, 2)[skipped:]
-
-        @pl.loop(0, HK, unroll=2)
-        def _(group):
-            k_rot = rotate(kv_ref[0, group, skipped:, :].astype(F32), cos_ref[skipped:, :], sin_ref[skipped:, :])
-            left = block_diagonal(k_rot.astype(BF16), kv_ref[1, group, skipped:, :])
-            k_rot_t = k_rot.T.astype(BF16)
-            near_t = jnp.concatenate([kt1_ref[group], kt0_ref[group]], axis=1)
-
-            def products(first):
-                both = dot_nt(left, qg_ref[group * (RATIO // PAIR) + first // PAIR])
-                return both[:used], both[used:]
-
-            def middle(first, scores, dprob):
-                at = slice(first * HD, (first + PAIR) * HD)
-                prob, _, total, scale = softmax_step(scores + bias, stat_ref, group, at, in_reach)
-                inverse = 1.0 / total
-                near_scale = scale * inverse
-                own_scale = near_scale * stat_ref[group, 3:4, at]
-                scale_ref[group, 0:1, at] = own_scale
-                prob = (prob * inverse).astype(BF16)
-                dscore = prob * (dprob - stat_ref[group, 2:3, at]).astype(BF16)
-                near_scale = near_scale.astype(BF16)
-                near_dscore = ds1_ref[group, :, at] * near_scale
-                own_dscore = ds0_ref[group, :, at] * own_scale.astype(BF16)
-                own_ref[group, :, at] = own_dscore
-                prob_buf[:used, at] = prob
-                prob_buf[used : used + rows, at] = prob1_ref[group, :, at] * near_scale
-                ds_buf[:used, at] = dscore
-                ds_buf[used : used + rows, at] = near_dscore
-                return dscore, jnp.concatenate([near_dscore, own_dscore], axis=0)
-
-            def finish(first, dscores):
-                dq = dot_nn(near_t, dscores[1]) + dot_nn(k_rot_t, dscores[0])
-                store_query_grad(dq_ref, group, first, dq, half_ref)
-
-            staged(products, middle, finish)
-            grads = key_products(qg_ref, group, ds_buf[: used + rows, :], prob_buf[: used + rows, :])
-            for which, grad in enumerate(grads):
-                ret1_ref[which, group] = grad[used:]
-                ret2_ref[which, group, skipped:, :] = grad[:used]
-                if skipped:
-                    ret2_ref[which, group, :skipped, :] = jnp.zeros((skipped, HD), BF16)
-
-    @pl.when(jnp.max(notes_ref[2:3, :]) > 0.0)
+        k_rot = rotate(kv_ref[0, group, skipped:, :].astype(F32), cos_ref[skipped:, :], sin_ref[skipped:, :])
+        left = block_diagonal(k_rot.astype(BF16), kv_ref[1, group, skipped:, :])
+        k_rot_t = k_rot.T.astype(BF16)
+        near_t = jnp.concatenate([kt1_ref[group], kt0_ref[group]], axis=1)
+
+        def products(tile):
+            both = dot_nt(left, qg_ref[group * TILES + tile])
+            return both[:used], both[used:]
+
+        def middle(tile, scores, dprob):
+            at = tile_columns(tile)
+            prob, _, total, scale = softmax_step(scores + bias, stat_ref, group, at, in_reach[tile // 2])
+            inverse = 1.0 / total
+            near_scale = scale * inverse
+            own_scale = near_scale * stat_ref[group, 3:4, at]
+            scale_ref[group, 0:1, at] = own_scale
+            prob = (prob * inverse).astype(BF16)
+            dscore = prob * (dprob - stat_ref[group, 2:3, at]).astype(BF16)
+            near_scale = near_scale.astype(BF16)
+            near_dscore = ds1_ref[group, :, at] * near_scale
+            own_dscore = ds0_ref[group, :, at] * own_scale.astype(BF16)
+            own_ref[group, :, at] = own_dscore
+            prob_buf[:used, at] = prob
+            prob_buf[used : used + rows, at] = prob1_ref[group, :, at] * near_scale
+            ds_buf[:used, at] = dscore
+            ds_buf[used : used + rows, at] = near_dscore
+            return dscore, jnp.concatenate([near_dscore, own_dscore], axis=0)
+
+        def finish(tile, dscores):
+            dq = dot_nn(near_t, dscores[1]) + dot_nn(k_rot_t, dscores[0])
+            store_query_grad(dq_ref, group, tile, dq, half_ref)
+
+        staged(tiles, products, middle, finish)
+        own_alone(
+            dq_ref, scale_ref, own_ref, ds0_ref, kt0_ref, stat_ref, half_ref, group, range(tiles, TILES)
+        )
+        columns = slice(0, tile_columns(tiles - 1).stop)
+        grads = key_products(qg_ref, group, tiles, ds_buf[: used + rows, columns], prob_buf[: used + rows, columns])
+        for which, grad in enumerate(grads):
+            ret1_ref[which, group] = grad[used:]
+            ret2_ref[which, group, skipped:, :] = grad[:used]
+            if skipped:
+                ret2_ref[which, group, :skipped, :] = jnp.zeros((skipped, HD), BF16)
+
+    @pl.when(goes_on(notes_ref))
     def _():
-        farthest = jnp.min(notes_ref[0:1, :])
-        pl.when(farthest >= -rows - rows // 2)(lambda: attend(rows // 2))
-        pl.when(farthest < -rows - rows // 2)(lambda: attend(0))
+        wide = high_reached(notes_ref)
+        pl.when(wide)(lambda: attend(rows // 2, TILES))
+        pl.when(jnp.logical_not(wide))(lambda: attend(0, TILES // 2))
 
 
 def own_kv_kernel(qg_ref, prob_ref, ds_ref, scale_ref, dk_ref, dv_ref):
@@ -437,13 +481,13 @@
         in_specs=[smem, vmem, vmem] + [hbm] * 5,
         out_specs=[vmem] * 13,
         out_shape=[
-            shape((8, rows), F32),
-            shape((HQ // PAIR, PAIR * rows, 2 * HD), BF16),
+            shape((8, QUAD * rows // 2), F32),
+            shape((HK * TILES, QUAD * rows // 2, 2 * HD), BF16),
             shape((HK, rows, RATIO * rows), BF16),
             shape((HK, rows, RATIO * rows), BF16),
             shape((HK, HD, rows), BF16),
             shape((HK, 8, RATIO * rows), F32),
-            shape((2, HALF, rows), F32),
+            shape((2, 2, HALF, QUAD * rows // 2), F32),
             shape((rows, HD), F32),
             shape((rows, HD), F32),
             shape((rows, HD), F32),

time: 39 us -> 37.4 us (0.959)
  starting transfers between devices: 15.3 us -> 13.6 us
    ppermute x5, starting transfers between devices: 15.3 us -> 13.6 us  [from_behind(): lax.ppermute(value, axis, [(source, source + steps) for source in range(i...]
  transfers between devices with their start and end apart: 5 -> 5, of which waited for: 3 -> 3; matrix products, arithmetic and copies ran while one was open for 0% -> 0% of each run, Pallas kernels for 24% -> 25%
where the time goes in v4:
time: 37.4 us; the launch traced here: 36.9 us
  starting transfers between devices  13.6 us (36%)
  Pallas kernels  11.3 us (30%)
  waiting for transfers between devices  11.3 us (30%)
  between operations  0.72 us (2%)
    ppermute x5, starting transfers between devices, from_behind(): lax.ppermute(value, axis, [(source, source + steps) for source in range(i...  13.6 us
    ppermute x5, waiting for transfers between devices, from_behind(): lax.ppermute(value, axis, [(source, source + steps) for source in range(i...  11.3 us
    pallas_call x1, Pallas kernels, shards(): pl.pallas_call(own_kernel, in_specs=[smem, vmem, vmem] + [hbm] * 5, out_s...  4.8 us
    pallas_call x1, Pallas kernels, shards(): pl.pallas_call(near_kernel, in_specs=[vmem] * 9, out_specs=[vmem] * 9, ou...  3.19 us
    pallas_call x1, Pallas kernels, shards(): pl.pallas_call(own_kv_kernel, in_specs=[vmem] * 4, out_specs=[vmem] * 2,...  1.18 us
    pallas_call x1, Pallas kernels, shards(): pl.pallas_call(sum_kernel, in_specs=[vmem] * 6 + [pl.BlockSpec(memory_spa...  1.08 us
    pallas_call x1, Pallas kernels, shards(): pl.pallas_call(pack_kernel, in_specs=[hbm, hbm], out_specs=vmem, out_shap...  0.95 us
  transfers between devices with their start and end apart: 5, of which 3 were waited for; matrix products, arithmetic and copies ran while one was open for 0% of the time, Pallas kernels for 25%

profile of v4, /device:TPU:14, one launch (start us, length us, event | category | flops | bytes accessed | tf_op | source)
XLA Modules:
  0.0 36.9 jit_solution(13005208149503878285)
XLA Ops:
  0.6 0.9 %pack_keys.1 = bf16[2,4,128,128]{3,2,1,0:T(8,128)(2,1)S(1)} custom-call(bf16[128,512]{1,0:T(8,128)(2,1)} %bitcast.10, bf16[128,512]{1,0:T(8,128)(2,1)} %bitcast.12), custom_call_target="tpu_custom_call" | custom-call | bytes 524288 | tf_op jit(solution)/shard_map/pack_keys/pallas_call | solution.py:466
  1.6 3.5 %collective-permute-start.1 = (bf16[2,4,128,128]{3,2,1,0:T(8,128)(2,1)S(1)}, bf16[2,4,128,128]{3,2,1,0:T(8,128)(2,1)S(1)}, u32[]{:S(2)}, u32[]{:S(2)}) collective-permute-start(bf16[2,4,128,128]{3,2,1,0:T(8,128)(2,1)S(1)} %pack_keys.1), channel_id=1, source_target_pairs={{0,4},{4,8},{8,12},{12,16},{16,20},{20,24},{24,28},{1,5},{5,9},{9,... | collective-permute-start | bytes 786440 | tf_op jit(solution)/shard_map/ppermute | solution.py:33
  5.0 3.5 %collective-permute-start = (bf16[2,4,128,128]{3,2,1,0:T(8,128)(2,1)S(1)}, bf16[2,4,128,128]{3,2,1,0:T(8,128)(2,1)S(1)}, u32[]{:S(2)}, u32[]{:S(2)}) collective-permute-start(bf16[2,4,128,128]{3,2,1,0:T(8,128)(2,1)S(1)} %pack_keys.1), channel_id=1, source_target_pairs={{0,8},{4,12},{8,16},{12,20},{16,24},{20,28},{1,9},{5,13},{9,17},{1... | collective-permute-start | bytes 786440 | tf_op jit(solution)/shard_map/ppermute | solution.py:33
  8.5 4.8 %own_block.1 = (f32[8,256]{1,0:T(8,128)S(1)}, bf16[16,256,256]{2,1,0:T(8,128)(2,1)S(1)}, bf16[4,128,1024]{2,1,0:T(8,128)(2,1)S(1)}, bf16[4,128,1024]{2,1,0:T(8,1...) custom-call(s32[1]{0:T(128)} %bitcast.first_ref, ...), custom_call_target="tpu_custom_call" | custom-call | flops 402653184 | bytes 9437184 | tf_op jit(solution)/shard_map/own_block/pallas_call | solution.py:479
  13.4 0.0 collective-permute-done.1.kv_ref
  13.4 3.2 %near_block.1 = (bf16[1,128,4096]{2,1,0:T(8,128)(2,1)S(1)}, bf16[2,4,128,128]{3,2,1,0:T(8,128)(2,1)S(1)}, bf16[2,4,128,128]{3,2,1,0:T(8,128)(2,1)S(1)}, f32[4,8,...) custom-call(f32[8,256]{1,0:T(8,128)S(1)} %get-tuple-element.37.notes, ...), custom_call_target="tpu_custom_call" | custom-call | flops 671088640 | bytes 9437184 | tf_op jit(solution)/shard_map/near_block/pallas_call | solution.py:518
  16.6 0.6 %collective-permute-done.kv_ref = bf16[2,4,128,128]{3,2,1,0:T(8,128)(2,1)S(1)} collective-permute-done((bf16[2,4,128,128]{3,2,1,0:T(8,128)(2,1)S(1)}, bf16[2,4,128,128]{3,2,1,0:T(8,128)(2,1)S(1)}, u32[]{:S(2)}, u32[]{:S(2)}) %collective-permute-start) | collective-permute-done | bytes 262176 | tf_op jit(solution)/shard_map/ppermute | solution.py:33
  17.1 0.1 far_block.1
  17.2 1.9 %collective-permute-start.4 = (bf16[1,128,4096]{2,1,0:T(8,128)(2,1)S(1)}, bf16[1,128,4096]{2,1,0:T(8,128)(2,1)S(1)}, u32[]{:S(2)}, u32[]{:S(2)}) collective-permute-start(bf16[1,128,4096]{2,1,0:T(8,128)(2,1)S(1)} %get-tuple-element.63), channel_id=1, source_target_pairs={{1,0},{2,1},{3,2},{5,4},{6,5},{7,6},{9,8},{10,9},{11,10},{13,12},{... | collective-permute-start | bytes 3145736 | tf_op jit(solution)/shard_map/ppermute | solution.py:33
  19.2 1.9 %collective-permute-start.2 = (bf16[2,4,128,128]{3,2,1,0:T(8,128)(2,1)S(1)}, bf16[2,4,128,128]{3,2,1,0:T(8,128)(2,1)S(1)}, u32[]{:S(2)}, u32[]{:S(2)}) collective-permute-start(bf16[2,4,128,128]{3,2,1,0:T(8,128)(2,1)S(1)} %get-tuple-element.59), channel_id=1, source_target_pairs={{8,0},{12,4},{16,8},{20,12},{24,16},{28,20},{9,1},{13,5},{17,9},{2... | collective-permute-start | bytes 786440 | tf_op jit(solution)/shard_map/ppermute | solution.py:33
  21.1 2.8 %collective-permute-start.3 = (bf16[2,4,128,128]{3,2,1,0:T(8,128)(2,1)S(1)}, bf16[2,4,128,128]{3,2,1,0:T(8,128)(2,1)S(1)}, u32[]{:S(2)}, u32[]{:S(2)}) collective-permute-start(bf16[2,4,128,128]{3,2,1,0:T(8,128)(2,1)S(1)} %get-tuple-element.60), channel_id=1, source_target_pairs={{4,0},{8,4},{12,8},{16,12},{20,16},{24,20},{28,24},{5,1},{9,5},{13... | collective-permute-start | bytes 786440 | tf_op jit(solution)/shard_map/ppermute | solution.py:33
  23.9 1.2 %own_keys.1 = (f32[4,128,128]{2,1,0:T(8,128)S(1)}, f32[4,128,128]{2,1,0:T(8,128)S(1)}) custom-call(bf16[16,256,256]{2,1,0:T(8,128)(2,1)S(1)} %get-tuple-element.35.qg_ref, bf16[4,128,1024]{2,1,0:T(8,128)(2,1)S(1)} %get-tuple-element.36.prob_ref, bf16[4,128,1024]{2,1,0:T(8,128)(2,1)S(1)} %get-tuple-element.55.ds_ref, ...), custom_call_target="tpu_custom_call" | custom-call | flops 268435456 | bytes 5242880 | tf_op jit(solution)/shard_map/own_keys/pallas_call | solution.py:552
  25.1 4.7 %collective-permute-done.2.ret2_ref = bf16[2,4,128,128]{3,2,1,0:T(8,128)(2,1)S(1)} collective-permute-done((bf16[2,4,128,128]{3,2,1,0:T(8,128)(2,1)S(1)}, bf16[2,4,128,128]{3,2,1,0:T(8,128)(2,1)S(1)}, u32[]{:S(2)}, u32[]{:S(2)}) %collective-permute-start.2) | collective-permute-done | bytes 262176 | tf_op jit(solution)/shard_map/ppermute | solution.py:33
  29.8 6.0 %collective-permute-done.3.ret1_ref = bf16[2,4,128,128]{3,2,1,0:T(8,128)(2,1)S(1)} collective-permute-done((bf16[2,4,128,128]{3,2,1,0:T(8,128)(2,1)S(1)}, bf16[2,4,128,128]{3,2,1,0:T(8,128)(2,1)S(1)}, u32[]{:S(2)}, u32[]{:S(2)}) %collective-permute-start.3) | collective-permute-done | bytes 262176 | tf_op jit(solution)/shard_map/ppermute | solution.py:33
  35.8 0.0 collective-permute-done.4.dq_ref
  35.8 1.1 %sum_keys.1 = (bf16[1,128,512]{2,1,0:T(8,128)(2,1)}, bf16[1,128,512]{2,1,0:T(8,128)(2,1)}, bf16[1,128,4096]{2,1,0:T(8,128)(2,1)}) custom-call(f32[4,128,128]{2,1,0:T(8,128)S(1)} %get-tuple-element.57.dk_ref, f32[4,128,128]{2,1,0:T(8,128)S(1)} %get-tuple-element.58.dv_ref, bf16[2,4,128,128]{3,2,1,0:T(8,128)(2,1)S(1)} %collective-permute-done.2.ret2_ref, ...), custom_call_target="tpu_custom_call" | custom-call | bytes 3145728 | tf_op jit(solution)/shard_map/sum_keys/pallas_call | solution.py:562
Async XLA Ops:
  1.6 11.8 %collective-permute-start.1 = (bf16[2,4,128,128]{3,2,1,0:T(8,128)(2,1)S(1)}, bf16[2,4,128,128]{3,2,1,0:T(8,128)(2,1)S(1)}, u32[]{:S(2)}, u32[]{:S(2)}) collective-permute-start(bf16[2,4,128,128]{3,2,1,0:T(8,128)(2,1)S(1)} %pack_keys.1), channel_id=1, source_target_pairs={{0,4},{4,8},{8,12},{12,16},{16,20},{20,24},{24,28},{1,5},{5,9},{9,... | collective-permute-start | bytes 786440 | tf_op jit(solution)/shard_map/ppermute | solution.py:33
  5.0 12.1 %collective-permute-start = (bf16[2,4,128,128]{3,2,1,0:T(8,128)(2,1)S(1)}, bf16[2,4,128,128]{3,2,1,0:T(8,128)(2,1)S(1)}, u32[]{:S(2)}, u32[]{:S(2)}) collective-permute-start(bf16[2,4,128,128]{3,2,1,0:T(8,128)(2,1)S(1)} %pack_keys.1), channel_id=1, source_target_pairs={{0,8},{4,12},{8,16},{12,20},{16,24},{20,28},{1,9},{5,13},{9,17},{1... | collective-permute-start | bytes 786440 | tf_op jit(solution)/shard_map/ppermute | solution.py:33
  17.2 18.6 %collective-permute-start.4 = (bf16[1,128,4096]{2,1,0:T(8,128)(2,1)S(1)}, bf16[1,128,4096]{2,1,0:T(8,128)(2,1)S(1)}, u32[]{:S(2)}, u32[]{:S(2)}) collective-permute-start(bf16[1,128,4096]{2,1,0:T(8,128)(2,1)S(1)} %get-tuple-element.63), channel_id=1, source_target_pairs={{1,0},{2,1},{3,2},{5,4},{6,5},{7,6},{9,8},{10,9},{11,10},{13,12},{... | collective-permute-start | bytes 3145736 | tf_op jit(solution)/shard_map/ppermute | solution.py:33
  19.2 10.7 %collective-permute-start.2 = (bf16[2,4,128,128]{3,2,1,0:T(8,128)(2,1)S(1)}, bf16[2,4,128,128]{3,2,1,0:T(8,128)(2,1)S(1)}, u32[]{:S(2)}, u32[]{:S(2)}) collective-permute-start(bf16[2,4,128,128]{3,2,1,0:T(8,128)(2,1)S(1)} %get-tuple-element.59), channel_id=1, source_target_pairs={{8,0},{12,4},{16,8},{20,12},{24,16},{28,20},{9,1},{13,5},{17,9},{2... | collective-permute-start | bytes 786440 | tf_op jit(solution)/shard_map/ppermute | solution.py:33
  21.1 14.7 %collective-permute-start.3 = (bf16[2,4,128,128]{3,2,1,0:T(8,128)(2,1)S(1)}, bf16[2,4,128,128]{3,2,1,0:T(8,128)(2,1)S(1)}, u32[]{:S(2)}, u32[]{:S(2)}) collective-permute-start(bf16[2,4,128,128]{3,2,1,0:T(8,128)(2,1)S(1)} %get-tuple-element.60), channel_id=1, source_target_pairs={{4,0},{8,4},{12,8},{16,12},{20,16},{24,20},{28,24},{5,1},{9,5},{13... | collective-permute-start | bytes 786440 | tf_op jit(solution)/shard_map/ppermute | solution.py:33

commit v5 on v4

--- a/solution.py
+++ b/solution.py
@@ -107,9 +107,8 @@
 
 def pack_kernel(k_hbm, v_hbm, kv_ref, arrived):
     copies = [
-        pltpu.make_async_copy(source.at[:, head_columns(group)], kv_ref.at[which, group], arrived.at[which, group])
+        pltpu.make_async_copy(source, kv_ref.at[which], arrived.at[which])
         for which, source in enumerate((k_hbm, v_hbm))
-        for group in range(HK)
     ]
     for copy in copies:
         copy.start()
@@ -274,7 +273,7 @@
     notes_ref, qg_ref, kv_ref, ds0_ref, kt0_ref, stat_ref, half_ref, cos_ref, sin_ref,
     dq_ref, ret2_ref, ret1_ref, scale_ref, own_ref, prob_ref, ds_ref, kt_ref, next_ref,
 ):
-    rows = kv_ref.shape[2]
+    rows = kv_ref.shape[1]
 
     def attend(last, tiles):
         in_reach = reached(notes_ref)
@@ -283,9 +282,9 @@
             one_group(last, tiles, in_reach, bias, group)
 
     def one_group(last, tiles, in_reach, bias, group):
-        k_rot = rotate(kv_ref[0, group].astype(F32), cos_ref[...], sin_ref[...])
+        k_rot = rotate(kv_ref[0, :, head_columns(group)].astype(F32), cos_ref[...], sin_ref[...])
         k_rot_t = k_rot.T.astype(BF16)
-        left = block_diagonal(k_rot.astype(BF16), kv_ref[1, group])
+        left = block_diagonal(k_rot.astype(BF16), kv_ref[1, :, head_columns(group)])
         both_t = jnp.concatenate([k_rot_t, kt0_ref[group]], axis=1)
 
         def products(tile):
@@ -345,8 +344,8 @@
     notes_ref, qg_ref, kv_ref, ds0_ref, kt0_ref, half_ref, cos_ref, sin_ref,
     prob1_ref, ds1_ref, kt1_ref, stat_ref, *refs,
 ):
-    dq_ref, ret2_ref, ret1_ref, scale_ref, own_ref, prob_buf, ds_buf = refs[5:]
-    rows = kv_ref.shape[2]
+    dq_ref, scale_ref, own_ref, prob_ref, ds_ref = refs[3:]
+    rows = kv_ref.shape[1]
 
     def attend(skipped, tiles):
         in_reach = reached(notes_ref)
@@ -356,8 +355,8 @@
 
     def one_group(skipped, tiles, in_reach, bias, group):
         used = rows - skipped
-        k_rot = rotate(kv_ref[0, group, skipped:, :].astype(F32), cos_ref[skipped:, :], sin_ref[skipped:, :])
-        left = block_diagonal(k_rot.astype(BF16), kv_ref[1, group, skipped:, :])
+        k_rot = rotate(kv_ref[0, skipped:, head_columns(group)].astype(F32), cos_ref[skipped:, :], sin_ref[skipped:, :])
+        left = block_diagonal(k_rot.astype(BF16), kv_ref[1, skipped:, head_columns(group)])
         k_rot_t = k_rot.T.astype(BF16)
         near_t = jnp.concatenate([kt1_ref[group], kt0_ref[group]], axis=1)
 
@@ -378,10 +377,10 @@
             near_dscore = ds1_ref[group, :, at] * near_scale
             own_dscore = ds0_ref[group, :, at] * own_scale.astype(BF16)
             own_ref[group, :, at] = own_dscore
-            prob_buf[:used, at] = prob
-            prob_buf[used : used + rows, at] = prob1_ref[group, :, at] * near_scale
-            ds_buf[:used, at] = dscore
-            ds_buf[used : used + rows, at] = near_dscore
+            prob_ref[group, :used, at] = prob
+            prob_ref[group, used : used + rows, at] = prob1_ref[group, :, at] * near_scale
+            ds_ref[group, :used, at] = dscore
+            ds_ref[group, used : used + rows, at] = near_dscore
             return dscore, jnp.concatenate([near_dscore, own_dscore], axis=0)
 
         def finish(tile, dscores):
@@ -392,19 +391,36 @@
         own_alone(
             dq_ref, scale_ref, own_ref, ds0_ref, kt0_ref, stat_ref, half_ref, group, range(tiles, TILES)
         )
-        columns = slice(0, tile_columns(tiles - 1).stop)
-        grads = key_products(qg_ref, group, tiles, ds_buf[: used + rows, columns], prob_buf[: used + rows, columns])
-        for which, grad in enumerate(grads):
-            ret1_ref[which, group] = grad[used:]
-            ret2_ref[which, group, skipped:, :] = grad[:used]
-            if skipped:
-                ret2_ref[which, group, :skipped, :] = jnp.zeros((skipped, HD), BF16)
-
+
+    far_cases(notes_ref, rows, attend)
+
+
+def far_cases(notes_ref, rows, attend):
     @pl.when(goes_on(notes_ref))
     def _():
         wide = high_reached(notes_ref)
         pl.when(wide)(lambda: attend(rows // 2, TILES))
         pl.when(jnp.logical_not(wide))(lambda: attend(0, TILES // 2))
+
+
+def far_keys_kernel(notes_ref, qg_ref, prob_ref, ds_ref, *refs):
+    ret2_ref, ret1_ref = refs[2:]
+    rows = ret1_ref.shape[2]
+
+    def attend(skipped, tiles):
+        used = rows - skipped
+        columns = slice(0, tile_columns(tiles - 1).stop)
+        for group in range(HK):
+            grads = key_products(
+                qg_ref, group, tiles, ds_ref[group, : used + rows, columns], prob_ref[group, : used + rows, columns]
+            )
+            for which, grad in enumerate(grads):
+                ret1_ref[which, group] = grad[used:]
+                ret2_ref[which, group, skipped:, :] = grad[:used]
+                if skipped:
+                    ret2_ref[which, group, :skipped, :] = jnp.zeros((skipped, HD), BF16)
+
+    far_cases(notes_ref, rows, attend)
 
 
 def own_kv_kernel(qg_ref, prob_ref, ds_ref, scale_ref, dk_ref, dv_ref):
@@ -467,8 +483,8 @@
         pack_kernel,
         in_specs=[hbm, hbm],
         out_specs=vmem,
-        out_shape=shape((2, HK, rows, HD), BF16),
-        scratch_shapes=[pltpu.SemaphoreType.DMA((2, HK))],
+        out_shape=shape((2, rows, kv_width), BF16),
+        scratch_shapes=[pltpu.SemaphoreType.DMA((2,))],
         compiler_params=params,
         cost_estimate=cost(0, 2**19),
         name="pack_keys",
@@ -508,46 +524,45 @@
         name="own_block",
     )(first_row, *(pltpu.with_memory_space_constraint(x, pltpu.HBM) for x in (fetch_list, doc_row)), *arguments)
 
-    results = [
-        shape((1, rows, HQ * HD), BF16),
-        shape((2, HK, rows, HD), BF16),
-        shape((2, HK, rows, HD), BF16),
-        shape((HK, 8, RATIO * rows), F32),
-        shape((HK, rows, RATIO * rows), BF16),
-    ]
-    *settled, prob1, ds1, k_near_t, stat1 = pl.pallas_call(
+    block = shape((HK, rows, RATIO * rows), BF16)
+    both_blocks = shape((HK, FETCH * rows, RATIO * rows), BF16)
+    statistics = shape((HK, 8, RATIO * rows), F32)
+    query_parts = [shape((1, rows, HQ * HD), BF16), statistics, block]
+    returns = [shape((2, HK, rows, HD), BF16)] * 2
+    dq, ret2, ret1, scale, ds_own, prob1, ds1, k_near_t, stat1 = pl.pallas_call(
         near_kernel,
         in_specs=[vmem] * 9,
         out_specs=[vmem] * 9,
-        out_shape=results
-        + [
-            shape((HK, rows, RATIO * rows), BF16),
-            shape((HK, rows, RATIO * rows), BF16),
-            shape((HK, HD, rows), BF16),
-            shape((HK, 8, RATIO * rows), F32),
-        ],
+        out_shape=[query_parts[0], *returns, *query_parts[1:], block, block, shape((HK, HD, rows), BF16), statistics],
         compiler_params=params,
         cost_estimate=cost(5 * block_flops, 9 * 2**20, HQ * rows * rows),
         name="near_block",
     )(notes, qg, kv1, ds0, k_own_t, stat, half, cos1, sin1)
 
-    dq, ret2, ret1, scale, ds_own = pl.pallas_call(
+    dq, scale, ds_own, prob12, ds12 = pl.pallas_call(
         far_kernel,
-        in_specs=[vmem] * 17,
+        in_specs=[vmem] * 15,
         out_specs=[vmem] * 5,
-        out_shape=results,
-        scratch_shapes=[
-            pltpu.VMEM((FETCH * rows, RATIO * rows), BF16),
-            pltpu.VMEM((FETCH * rows, RATIO * rows), BF16),
-        ],
-        input_output_aliases={12 + i: i for i in range(5)},
+        out_shape=[*query_parts, both_blocks, both_blocks],
+        input_output_aliases={12: 0, 13: 1, 14: 2},
         compiler_params=params,
-        cost_estimate=cost(5 * block_flops, 9 * 2**20, HQ * rows * rows),
+        cost_estimate=cost(3 * block_flops, 9 * 2**20, HQ * rows * rows),
         name="far_block",
-    )(notes, qg, kv2, ds0, k_own_t, half, cos2, sin2, prob1, ds1, k_near_t, stat1, *settled)
+    )(notes, qg, kv2, ds0, k_own_t, half, cos2, sin2, prob1, ds1, k_near_t, stat1, dq, scale, ds_own)
+    handed = from_behind(dq, "section", -1)
+
+    ret2, ret1 = pl.pallas_call(
+        far_keys_kernel,
+        in_specs=[vmem] * 6,
+        out_specs=[vmem] * 2,
+        out_shape=returns,
+        input_output_aliases={4: 0, 5: 1},
+        compiler_params=params,
+        cost_estimate=cost(4 * block_flops, 9 * 2**20),
+        name="far_keys",
+    )(notes, qg, prob12, ds12, ret2, ret1)
     arrived1 = from_behind(ret1, "ctx", -1)
     arrived2 = from_behind(ret2, "ctx", -2)
-    dq_next = from_behind(dq, "section", -1)
 
     dk0, dv0 = pl.pallas_call(
         own_kv_kernel,
@@ -576,7 +591,7 @@
         compiler_params=params,
         cost_estimate=cost(0, 3 * 2**20),
         name="sum_keys",
-    )(dk0, dv0, arrived2, arrived1, cos, sin, dq_next)
+    )(dk0, dv0, arrived2, arrived1, cos, sin, handed)
     return (handed_grad, key_grad, value_grad)
 
 

time: 37.4 us -> 37.8 us (1.011)
  starting transfers between devices: 13.6 us -> 14 us
    ppermute x5, starting transfers between devices: 13.6 us -> 14 us  [from_behind(): lax.ppermute(value, axis, [(source, source + steps) for source in range(i...]
where the time goes in v5:
time: 37.8 us; the launch traced here: 37.4 us
  starting transfers between devices  14 us (37%)
  Pallas kernels  11.5 us (30%)
  waiting for transfers between devices  11.2 us (30%)
  between operations  0.73 us (2%)
    ppermute x5, starting transfers between devices, from_behind(): lax.ppermute(value, axis, [(source, source + steps) for source in range(i...  14 us
    ppermute x5, waiting for transfers between devices, from_behind(): lax.ppermute(value, axis, [(source, source + steps) for source in range(i...  11.2 us
    pallas_call x1, Pallas kernels, shards(): pl.pallas_call(own_kernel, in_specs=[smem, vmem, vmem] + [hbm] * 5, out_s...  4.79 us
    pallas_call x1, Pallas kernels, shards(): pl.pallas_call(near_kernel, in_specs=[vmem] * 9, out_specs=[vmem] * 9, ou...  3.21 us
    pallas_call x1, Pallas kernels, shards(): pl.pallas_call(own_kv_kernel, in_specs=[vmem] * 4, out_specs=[vmem] * 2,...  1.17 us
    pallas_call x1, Pallas kernels, shards(): pl.pallas_call(sum_kernel, in_specs=[vmem] * 6 + [pl.BlockSpec(memory_spa...  1.08 us
    pallas_call x1, Pallas kernels, shards(): pl.pallas_call(pack_kernel, in_specs=[hbm, hbm], out_specs=vmem, out_shap...  0.99 us
  transfers between devices with their start and end apart: 5, of which 3 were waited for; matrix products, arithmetic and copies ran while one was open for 0% of the time, Pallas kernels for 25%

profile of v5, /device:TPU:14, one launch (start us, length us, event | category | flops | bytes accessed | tf_op | source)
XLA Modules:
  0.0 37.4 jit_solution(1971993683788546507)
XLA Ops:
  0.6 1.0 %pack_keys.1 = bf16[2,128,512]{2,1,0:T(8,128)(2,1)S(1)} custom-call(bf16[128,512]{1,0:T(8,128)(2,1)} %bitcast.10, bf16[128,512]{1,0:T(8,128)(2,1)} %bitcast.12), custom_call_target="tpu_custom_call" | custom-call | bytes 524288 | tf_op jit(solution)/shard_map/pack_keys/pallas_call | solution.py:482
  1.6 3.5 %collective-permute-start.1 = (bf16[2,128,512]{2,1,0:T(8,128)(2,1)S(1)}, bf16[2,128,512]{2,1,0:T(8,128)(2,1)S(1)}, u32[]{:S(2)}, u32[]{:S(2)}) collective-permute-start(bf16[2,128,512]{2,1,0:T(8,128)(2,1)S(1)} %pack_keys.1), channel_id=1, source_target_pairs={{0,4},{4,8},{8,12},{12,16},{16,20},{20,24},{24,28},{1,5},{5,9},{9,... | collective-permute-start | bytes 786440 | tf_op jit(solution)/shard_map/ppermute | solution.py:33
  5.1 3.5 %collective-permute-start = (bf16[2,128,512]{2,1,0:T(8,128)(2,1)S(1)}, bf16[2,128,512]{2,1,0:T(8,128)(2,1)S(1)}, u32[]{:S(2)}, u32[]{:S(2)}) collective-permute-start(bf16[2,128,512]{2,1,0:T(8,128)(2,1)S(1)} %pack_keys.1), channel_id=1, source_target_pairs={{0,8},{4,12},{8,16},{12,20},{16,24},{20,28},{1,9},{5,13},{9,17},{1... | collective-permute-start | bytes 786440 | tf_op jit(solution)/shard_map/ppermute | solution.py:33
  8.6 4.8 %own_block.1 = (f32[8,256]{1,0:T(8,128)S(1)}, bf16[16,256,256]{2,1,0:T(8,128)(2,1)S(1)}, bf16[4,128,1024]{2,1,0:T(8,128)(2,1)S(1)}, bf16[4,128,1024]{2,1,0:T(8,1...) custom-call(s32[1]{0:T(128)} %bitcast.first_ref, ...), custom_call_target="tpu_custom_call" | custom-call | flops 402653184 | bytes 9437184 | tf_op jit(solution)/shard_map/own_block/pallas_call | solution.py:495
  13.4 0.0 collective-permute-done.1.kv_ref
  13.4 3.2 %near_block.1 = (bf16[1,128,4096]{2,1,0:T(8,128)(2,1)S(1)}, bf16[2,4,128,128]{3,2,1,0:T(8,128)(2,1)S(1)}, bf16[2,4,128,128]{3,2,1,0:T(8,128)(2,1)S(1)}, f32[4,8,...) custom-call(f32[8,256]{1,0:T(8,128)S(1)} %get-tuple-element.39.notes, ...), custom_call_target="tpu_custom_call" | custom-call | flops 671088640 | bytes 9437184 | tf_op jit(solution)/shard_map/near_block/pallas_call | solution.py:532
  16.6 0.5 %collective-permute-done.kv_ref = bf16[2,128,512]{2,1,0:T(8,128)(2,1)S(1)} collective-permute-done((bf16[2,128,512]{2,1,0:T(8,128)(2,1)S(1)}, bf16[2,128,512]{2,1,0:T(8,128)(2,1)S(1)}, u32[]{:S(2)}, u32[]{:S(2)}) %collective-permute-start) | collective-permute-done | bytes 262176 | tf_op jit(solution)/shard_map/ppermute | solution.py:33
  17.2 0.1 far_block.1
  17.3 1.9 %collective-permute-start.4 = (bf16[1,128,4096]{2,1,0:T(8,128)(2,1)S(1)}, bf16[1,128,4096]{2,1,0:T(8,128)(2,1)S(1)}, u32[]{:S(2)}, u32[]{:S(2)}) collective-permute-start(bf16[1,128,4096]{2,1,0:T(8,128)(2,1)S(1)} %get-tuple-element.67), channel_id=1, source_target_pairs={{1,0},{2,1},{3,2},{5,4},{6,5},{7,6},{9,8},{10,9},{11,10},{13,12},{... | collective-permute-start | bytes 3145736 | tf_op jit(solution)/shard_map/ppermute | solution.py:33
  19.2 0.1 far_keys.1
  19.3 1.9 %collective-permute-start.2 = (bf16[2,4,128,128]{3,2,1,0:T(8,128)(2,1)S(1)}, bf16[2,4,128,128]{3,2,1,0:T(8,128)(2,1)S(1)}, u32[]{:S(2)}, u32[]{:S(2)}) collective-permute-start(bf16[2,4,128,128]{3,2,1,0:T(8,128)(2,1)S(1)} %get-tuple-element.63), channel_id=1, source_target_pairs={{8,0},{12,4},{16,8},{20,12},{24,16},{28,20},{9,1},{13,5},{17,9},{2... | collective-permute-start | bytes 786440 | tf_op jit(solution)/shard_map/ppermute | solution.py:33
  21.3 3.2 %collective-permute-start.3 = (bf16[2,4,128,128]{3,2,1,0:T(8,128)(2,1)S(1)}, bf16[2,4,128,128]{3,2,1,0:T(8,128)(2,1)S(1)}, u32[]{:S(2)}, u32[]{:S(2)}) collective-permute-start(bf16[2,4,128,128]{3,2,1,0:T(8,128)(2,1)S(1)} %get-tuple-element.64), channel_id=1, source_target_pairs={{4,0},{8,4},{12,8},{16,12},{20,16},{24,20},{28,24},{5,1},{9,5},{13... | collective-permute-start | bytes 786440 | tf_op jit(solution)/shard_map/ppermute | solution.py:33
  24.5 1.2 %own_keys.1 = (f32[4,128,128]{2,1,0:T(8,128)S(1)}, f32[4,128,128]{2,1,0:T(8,128)S(1)}) custom-call(bf16[16,256,256]{2,1,0:T(8,128)(2,1)S(1)} %get-tuple-element.37.qg_ref, bf16[4,128,1024]{2,1,0:T(8,128)(2,1)S(1)} %get-tuple-element.38.prob_ref, bf16[4,128,1024]{2,1,0:T(8,128)(2,1)S(1)} %get-tuple-element.55.ds_ref, ...), custom_call_target="tpu_custom_call" | custom-call | flops 268435456 | bytes 5242880 | tf_op jit(solution)/shard_map/own_keys/pallas_call | solution.py:567
  25.7 7.9 %collective-permute-done.2.ret2_ref = bf16[2,4,128,128]{3,2,1,0:T(8,128)(2,1)S(1)} collective-permute-done((bf16[2,4,128,128]{3,2,1,0:T(8,128)(2,1)S(1)}, bf16[2,4,128,128]{3,2,1,0:T(8,128)(2,1)S(1)}, u32[]{:S(2)}, u32[]{:S(2)}) %collective-permute-start.2) | collective-permute-done | bytes 262176 | tf_op jit(solution)/shard_map/ppermute | solution.py:33
  33.6 2.8 %collective-permute-done.3.ret1_ref = bf16[2,4,128,128]{3,2,1,0:T(8,128)(2,1)S(1)} collective-permute-done((bf16[2,4,128,128]{3,2,1,0:T(8,128)(2,1)S(1)}, bf16[2,4,128,128]{3,2,1,0:T(8,128)(2,1)S(1)}, u32[]{:S(2)}, u32[]{:S(2)}) %collective-permute-start.3) | collective-permute-done | bytes 262176 | tf_op jit(solution)/shard_map/ppermute | solution.py:33
  36.4 0.0 collective-permute-done.4.dq_ref
  36.4 1.1 %sum_keys.1 = (bf16[1,128,512]{2,1,0:T(8,128)(2,1)}, bf16[1,128,512]{2,1,0:T(8,128)(2,1)}, bf16[1,128,4096]{2,1,0:T(8,128)(2,1)}) custom-call(f32[4,128,128]{2,1,0:T(8,128)S(1)} %get-tuple-element.57.dk_ref, f32[4,128,128]{2,1,0:T(8,128)S(1)} %get-tuple-element.58.dv_ref, bf16[2,4,128,128]{3,2,1,0:T(8,128)(2,1)S(1)} %collective-permute-done.2.ret2_ref, ...), custom_call_target="tpu_custom_call" | custom-call | bytes 3145728 | tf_op jit(solution)/shard_map/sum_keys/pallas_call | solution.py:577
Async XLA Ops:
  1.6 11.8 %collective-permute-start.1 = (bf16[2,128,512]{2,1,0:T(8,128)(2,1)S(1)}, bf16[2,128,512]{2,1,0:T(8,128)(2,1)S(1)}, u32[]{:S(2)}, u32[]{:S(2)}) collective-permute-start(bf16[2,128,512]{2,1,0:T(8,128)(2,1)S(1)} %pack_keys.1), channel_id=1, source_target_pairs={{0,4},{4,8},{8,12},{12,16},{16,20},{20,24},{24,28},{1,5},{5,9},{9,... | collective-permute-start | bytes 786440 | tf_op jit(solution)/shard_map/ppermute | solution.py:33
  5.1 12.1 %collective-permute-start = (bf16[2,128,512]{2,1,0:T(8,128)(2,1)S(1)}, bf16[2,128,512]{2,1,0:T(8,128)(2,1)S(1)}, u32[]{:S(2)}, u32[]{:S(2)}) collective-permute-start(bf16[2,128,512]{2,1,0:T(8,128)(2,1)S(1)} %pack_keys.1), channel_id=1, source_target_pairs={{0,8},{4,12},{8,16},{12,20},{16,24},{20,28},{1,9},{5,13},{9,17},{1... | collective-permute-start | bytes 786440 | tf_op jit(solution)/shard_map/ppermute | solution.py:33
  17.3 19.1 %collective-permute-start.4 = (bf16[1,128,4096]{2,1,0:T(8,128)(2,1)S(1)}, bf16[1,128,4096]{2,1,0:T(8,128)(2,1)S(1)}, u32[]{:S(2)}, u32[]{:S(2)}) collective-permute-start(bf16[1,128,4096]{2,1,0:T(8,128)(2,1)S(1)} %get-tuple-element.67), channel_id=1, source_target_pairs={{1,0},{2,1},{3,2},{5,4},{6,5},{7,6},{9,8},{10,9},{11,10},{13,12},{... | collective-permute-start | bytes 3145736 | tf_op jit(solution)/shard_map/ppermute | solution.py:33
  19.3 14.2 %collective-permute-start.2 = (bf16[2,4,128,128]{3,2,1,0:T(8,128)(2,1)S(1)}, bf16[2,4,128,128]{3,2,1,0:T(8,128)(2,1)S(1)}, u32[]{:S(2)}, u32[]{:S(2)}) collective-permute-start(bf16[2,4,128,128]{3,2,1,0:T(8,128)(2,1)S(1)} %get-tuple-element.63), channel_id=1, source_target_pairs={{8,0},{12,4},{16,8},{20,12},{24,16},{28,20},{9,1},{13,5},{17,9},{2... | collective-permute-start | bytes 786440 | tf_op jit(solution)/shard_map/ppermute | solution.py:33
  21.3 15.1 %collective-permute-start.3 = (bf16[2,4,128,128]{3,2,1,0:T(8,128)(2,1)S(1)}, bf16[2,4,128,128]{3,2,1,0:T(8,128)(2,1)S(1)}, u32[]{:S(2)}, u32[]{:S(2)}) collective-permute-start(bf16[2,4,128,128]{3,2,1,0:T(8,128)(2,1)S(1)} %get-tuple-element.64), channel_id=1, source_target_pairs={{4,0},{8,4},{12,8},{16,12},{20,16},{24,20},{28,24},{5,1},{9,5},{13... | collective-permute-start | bytes 786440 | tf_op jit(solution)/shard_map/ppermute | solution.py:33
